TPU v7x, 256 devices: a whole 4x4x8 slice. The times are simulated.
256 devices in a mesh: row: 16 (over y_hi, z), col: 16 (over x, y_lo, core).
Axes of the slice: x: 4, y: 4 (y_hi: 2, y_lo: 2; y = y_hi * 2 + y_lo), z: 8, core: 2. Of those that a mesh axis runs over, the one named last changes fastest.
Arguments:
- stack_embedding: bfloat16 [128, 640, 256], P('row', 'col'), may hold values from -6 to 6
- pair_representation: bfloat16 [640, 640, 128], P('row', 'col'), may hold values from -8 to 8
- mixing_entry_coefficients: bfloat16 [256, 1024], replicated, may hold values from -0.375 to 0.375
- mixing_final_coefficients: bfloat16 [256, 256], replicated, may hold values from -1 to 1
- pair_bias_matrix: bfloat16 [128, 8], replicated, may hold values from -4 to 4
- tensor_side_coefficients: bfloat16 [256, 64], replicated, may hold values from -0.375 to 0.375
- outer_output_weight: bfloat16 [1024, 128], replicated, may hold values from -1 to 1
- triangle_projection_weight: bfloat16 [128, 640], replicated, may hold values from -0.5 to 0.5
- triangle_output_weight: bfloat16 [128, 128], replicated, may hold values from -0.5 to 0.5
Outputs:
- stack_embedding_updated: bfloat16 [128, 640, 256], P('row', 'col')
- pair_state_next: bfloat16 [640, 640, 128], P('row', 'col')
All inputs are finite; a program needn't handle non-finite values.
Results may differ from a plain program's by a relative error of at most 0.015.
Values may be sent and summed in bfloat16 or wider, within the bound.
A program may use at most 128 MiB of HBM per device.

v0:
```python
import jax
import jax.numpy as jnp
from jax import lax
from jax.sharding import Mesh
from jax.sharding import PartitionSpec as P

ROW = ("row_0", "row_1")


epsilon = 1e-05


def laid_out(blocks, dim):
    blocks = jnp.moveaxis(blocks, 0, dim)
    dims = blocks.shape
    return blocks.reshape(*dims[:dim], dims[dim] * dims[dim + 1], *dims[dim + 2 :])


def copy_for_each(x, axis):
    copies = jnp.broadcast_to(x, (lax.axis_size(axis), *x.shape))
    return lax.all_to_all(copies, axis, split_axis=0, concat_axis=0, tiled=True)


def gathered_copies(x, axis, dim):
    return laid_out(copy_for_each(x, axis), dim)


def in_one_piece(arrays, axis, dim, along):
    both = jnp.concatenate(arrays, axis=along)
    filled, at, outs = (lax.all_gather(both, axis, axis=dim, tiled=True), 0, [])
    for a in arrays:
        outs.append(lax.slice_in_dim(filled, at, at + a.shape[along], axis=along))
        at += a.shape[along]
    return tuple(outs)


def all_blocks(x, axes, sequence):
    blocks = x
    for k in sequence:
        blocks = lax.all_gather(blocks, axes[k])
    done = sequence[::-1]
    back = [done.index(k) for k in range(len(axes))]
    blocks = blocks.transpose(*back, *range(len(axes), blocks.ndim))
    return blocks.reshape(-1, *x.shape)


def whole_of(x, axes, sequence, dim):
    return laid_out(all_blocks(x, axes, sequence), dim)


def standardize_features(inputs):
    inputs = inputs.astype(jnp.float32)
    center = inputs - jnp.mean(inputs, axis=-1, keepdims=True)
    spread = jnp.mean(center * center, axis=-1, keepdims=True)
    return center * lax.rsqrt(spread + epsilon)


def shards(
    stack_embedding,
    pair_representation,
    mixing_entry_coefficients,
    mixing_final_coefficients,
    pair_bias_matrix,
    tensor_side_coefficients,
    outer_output_weight,
    triangle_projection_weight,
    triangle_output_weight,
):
    sequences_per_device, residues_per_device, alignment_channels = stack_embedding.shape
    rows_dev = pair_representation.shape[0]
    pair_width = pair_representation.shape[2]
    number_heads = pair_bias_matrix.shape[1]
    head_channels = alignment_channels // number_heads
    outer_width = tensor_side_coefficients.shape[1] // 2
    row_count = lax.axis_size(ROW)
    seq_total = sequences_per_device * row_count
    row_index = lax.axis_index(ROW)
    normalized_input = (
        standardize_features(stack_embedding).astype(jnp.bfloat16).reshape(-1, alignment_channels)
    )
    mapped_lines = jnp.dot(
        normalized_input, mixing_entry_coefficients, preferred_element_type=jnp.float32
    )
    stack_probe_vectors = (
        (mapped_lines[:, :alignment_channels] * head_channels ** (-0.5))
        .astype(jnp.bfloat16)
        .reshape(sequences_per_device, residues_per_device, number_heads, head_channels)
    )
    stack_lookup_vectors = (
        mapped_lines[:, alignment_channels : 2 * alignment_channels]
        .astype(jnp.bfloat16)
        .reshape(sequences_per_device, residues_per_device, alignment_channels)
    )
    stack_content_vectors = (
        mapped_lines[:, 2 * alignment_channels : 3 * alignment_channels]
        .astype(jnp.bfloat16)
        .reshape(sequences_per_device, residues_per_device, alignment_channels)
    )
    sigmoid_factors = jax.nn.sigmoid(mapped_lines[:, 3 * alignment_channels :]).reshape(
        sequences_per_device, residues_per_device, alignment_channels
    )
    pair_normed = standardize_features(pair_representation).astype(jnp.bfloat16)
    bias_local = jnp.einsum(
        "ijc,ch->hij", pair_normed, pair_bias_matrix, preferred_element_type=jnp.float32
    ).astype(jnp.bfloat16)
    bias_all = gathered_copies(bias_local, ROW, 1)
    bias_query = lax.all_to_all(bias_all, "col", split_axis=1, concat_axis=2, tiled=True)
    best_score = jnp.full(
        (sequences_per_device, number_heads, residues_per_device), -1e30, jnp.float32
    )
    received_keys, received_values = in_one_piece(
        (stack_lookup_vectors, stack_content_vectors), "col", 1, 0
    )
    key_count = received_keys.shape[1]
    received_keys = received_keys.reshape(
        sequences_per_device, key_count, number_heads, head_channels
    )
    received_values = received_values.reshape(
        sequences_per_device, key_count, number_heads, head_channels
    )
    bias_piece = bias_query.astype(jnp.float32)
    scores = (
        jnp.einsum(
            "yeca,yica->ycei",
            stack_probe_vectors,
            received_keys,
            preferred_element_type=jnp.float32,
        )
        + bias_piece[None]
    )
    next_best = jnp.maximum(best_score, jnp.max(scores, axis=-1))
    weights = jnp.exp(scores - next_best[..., None])
    next_sum = jnp.sum(weights, axis=-1)
    update = jnp.einsum(
        "shqk,skhd->sqhd",
        weights.astype(jnp.bfloat16),
        received_values,
        preferred_element_type=jnp.float32,
    )
    weighted_mixture = (update / jnp.transpose(next_sum, (0, 2, 1))[..., None]).reshape(
        sequences_per_device, residues_per_device, alignment_channels
    )
    scaled_mixture = (sigmoid_factors * weighted_mixture).astype(jnp.bfloat16)
    stack_increment = jnp.dot(
        scaled_mixture.reshape(-1, alignment_channels),
        mixing_final_coefficients,
        preferred_element_type=jnp.float32,
    ).reshape(sequences_per_device, residues_per_device, alignment_channels)
    stack_embedding_updated = (stack_embedding.astype(jnp.float32) + stack_increment).astype(
        jnp.bfloat16
    )
    tensor_standardized = (
        standardize_features(stack_embedding_updated)
        .astype(jnp.bfloat16)
        .reshape(-1, alignment_channels)
    )
    sides = jnp.dot(
        tensor_standardized, tensor_side_coefficients, preferred_element_type=jnp.float32
    ).astype(jnp.bfloat16)
    sides = sides.reshape(sequences_per_device, residues_per_device, 2 * outer_width)
    left_side = sides[..., :outer_width]
    right_side = sides[..., outer_width:]
    left_wide = lax.all_gather(left_side, "col", axis=1, tiled=True)
    left_every, right_all = (
        lax.all_gather(left_wide, ROW, axis=0, tiled=True),
        lax.all_gather(right_side, ROW, axis=0, tiled=True),
    )
    left_all = lax.dynamic_slice_in_dim(left_every, row_index * rows_dev, rows_dev, 1)
    products = jnp.einsum("sic,sjd->ijcd", left_all, right_all, preferred_element_type=jnp.float32)
    averaged = (products * (1.0 / seq_total)).astype(jnp.bfloat16)
    outer_update = jnp.dot(
        averaged.reshape(-1, outer_width * outer_width),
        outer_output_weight,
        preferred_element_type=jnp.float32,
    )
    pair_mid = (
        pair_representation.astype(jnp.float32)
        + outer_update.reshape(rows_dev, residues_per_device, pair_width)
    ).astype(jnp.bfloat16)
    tri_normed = standardize_features(pair_mid).astype(jnp.bfloat16).reshape(-1, pair_width)
    tri_parts = jnp.dot(
        tri_normed, triangle_projection_weight, preferred_element_type=jnp.float32
    ).reshape(rows_dev, residues_per_device, 5 * pair_width)
    left_edge = (
        jax.nn.sigmoid(tri_parts[..., pair_width : 2 * pair_width]) * tri_parts[..., :pair_width]
    ).astype(jnp.bfloat16)
    right_edge = (
        jax.nn.sigmoid(tri_parts[..., 3 * pair_width : 4 * pair_width])
        * tri_parts[..., 2 * pair_width : 3 * pair_width]
    ).astype(jnp.bfloat16)
    out_gate = jax.nn.sigmoid(tri_parts[..., 4 * pair_width :])
    right_parts = lax.all_to_all(
        lax.all_to_all(right_edge, ROW, split_axis=2, concat_axis=0, tiled=True),
        "col",
        split_axis=0,
        concat_axis=1,
        tiled=True,
    )
    right_query = whole_of(right_parts, ROW, (0, 1), 2)
    arrived = lax.all_gather(left_edge, "col", axis=1, tiled=True)
    summed = jnp.einsum("ikc,jkc->ijc", arrived, right_query, preferred_element_type=jnp.float32)
    tri_ln = standardize_features(summed).astype(jnp.bfloat16)
    tri_update = jnp.dot(
        tri_ln.reshape(-1, pair_width), triangle_output_weight, preferred_element_type=jnp.float32
    ).reshape(rows_dev, residues_per_device, pair_width)
    pair_state_next = (pair_mid.astype(jnp.float32) + out_gate * tri_update).astype(jnp.bfloat16)
    return (stack_embedding_updated, pair_state_next)


def solution(mesh):
    finer = Mesh(mesh.devices.reshape(2, 8, mesh.shape["col"]), ("row_0", "row_1", "col"))
    in_specs = (P(ROW, "col", None), P(ROW, "col", None), P(), P(), P(), P(), P(), P(), P())
    out_specs = (P(ROW, "col", None), P(ROW, "col", None))
    return jax.shard_map(
        shards, mesh=finer, in_specs=in_specs, out_specs=out_specs, check_vma=False
    )
```

profile of v0, /device:TPU:8, one launch (start us, length us, event | category | flops | bytes accessed | tf_op | source)
XLA Modules:
  0.0 408.2 jit_solution(6786454003943087592)
XLA Ops:
  7.2 1.1 convert_reduce_fusion.1
  8.4 1.1 fusion.55
  9.5 1.1 fusion.56
  10.6 1.5 fusion.75
  12.1 0.8 pad_maximum_fusion
  13.2 0.5 fusion.30
  13.7 0.6 fusion.24
  14.7 2.0 reshape.155
  16.7 24.6 %all_to_all.47 = bf16[16,2,6400]{2,1,0:T(2,128)(2,1)S(1)} all-to-all(bf16[16,2,6400]{2,1,0:T(2,128)(2,1)S(1)} %reshape.155), channel_id=1, replica_groups=mesh['row_0'=2,'row_1'=8,'col'=16] {'row_0','row_1'}, dimensions={0} | all-to-all | bytes 819200 | tf_op jit(solution)/shard_map/all_to_all | solution.py:21
  41.3 2.0 reshape.156
  43.5 0.9 copy.180
  44.4 2.8 reshape.157
  47.2 5.8 %all-to-all-start.1 = ((bf16[16,2,6400]{2,1,0:T(2,128)(2,1)}), bf16[16,2,6400]{2,1,0:T(2,128)(2,1)S(1)}, u32[]{:S(2)}, u32[]{:S(2)}) async-start(bf16[16,2,6400]{2,1,0:T(2,128)(2,1)} %reshape.157), calls=%async_computation.1 | async-start | bytes 819200 | tf_op jit(solution)/shard_map/all_to_all | solution.py:107
  53.0 0.6 all-gather.8.cloned.1.call-start
  53.5 1.0 fusion.59
  54.5 1.1 reshape.153
  55.7 8.2 %all-to-all-done.1 = bf16[16,2,6400]{2,1,0:T(2,128)(2,1)S(1)} async-done(((bf16[16,2,6400]{2,1,0:T(2,128)(2,1)}), bf16[16,2,6400]{2,1,0:T(2,128)(2,1)S(1)}, u32[]{:S(2)}, u32[]{:S(2)}) %all-to-all-start.1) | async-done | bytes 409632 | tf_op jit(solution)/shard_map/all_to_all | solution.py:107
  63.9 2.0 reshape.158
  66.0 1.2 copy.146
  67.2 1.8 reshape.144
  69.0 2.8 copy.147
  71.7 3.4 reshape.143
  75.1 4.4 %fusion.72 = (bf16[8,640,256]{2,1,0:T(8,128)(2,1)}, bf16[8,640,256]{2,1,0:T(8,128)(2,1)S(1)}) fusion(bf16[16,640,256]{2,1,0:T(8,128)(2,1)} %all-gather.6.cloned.1.call-done), kind=kLoop, calls=%fused_computation.100 | loop fusion | bytes 10485760 | tf_op jit(solution)/shard_map/slice | solution.py:32
  79.6 4.4 %copy.140 = bf16[8,640,256]{1,2,0:T(8,128)(2,1)} copy(bf16[8,640,256]{2,1,0:T(8,128)(2,1)} %get-tuple-element.10) | data formatting | bytes 5242880 | tf_op jit(solution)/shard_map/slice | solution.py:32
  84.0 2.6 copy.138
  86.5 3.4 add_reduce_fusion
  90.0 1.7 fusion
  91.8 1.5 fusion.25
  93.3 0.5 copy.181
  93.8 0.4 reshape.154
  94.2 1.1 fusion.65
  96.4 22.2 %all_gather.29 = bf16[8,640,32]{2,1,0:T(8,128)(2,1)S(1)} all-gather(bf16[8,40,32]{2,1,0:T(8,128)(2,1)S(1)} %get-tuple-element.16), channel_id=1, replica_groups=mesh['row_0'=2,'row_1'=8,'col'=16] {'col'}, dimensions={1}, use_global_device_ids=true | all-gather | bytes 348160 | tf_op jit(solution)/shard_map/all_gather | solution.py:163
  118.6 1.2 copy.152
  119.9 50.2 %all_gather.28 = bf16[128,40,32]{2,0,1:T(8,128)(2,1)S(1)} all-gather(bf16[8,40,32]{2,0,1:T(8,128)(2,1)S(1)} %copy.188), channel_id=1, replica_groups=mesh['row_0'=2,'row_1'=8,'col'=16] {'row_0','row_1'}, dimensions={0}, use_global_device_ids=true | all-gather | bytes 348160 | tf_op jit(solution)/shard_map/all_gather | solution.py:166
  170.2 57.4 %all-gather.8.cloned.1.call-done = bf16[128,640,32]{1,2,0:T(8,128)(2,1)} async-done(((bf16[8,640,32]{1,2,0:T(8,128)(2,1)}), bf16[128,640,32]{1,2,0:T(8,128)(2,1)}) %all-gather.8.cloned.1.call-update) | async-done | bytes 5242896 | tf_op jit(solution)/shard_map/all_gather | solution.py:165
  227.5 2.0 constant_dynamic-slice_fusion
  229.5 1.1 copy.189
  230.6 5.8 %multiply_convert_fusion = bf16[40,32,40,32]{2,1,3,0:T(8,128)(2,1)S(1)} fusion(bf16[128,40,32]{2,0,1:T(8,128)(2,1)S(1)} %all_gather.28, bf16[128,40,32]{0,1,2:T(8,128)(2,1)S(1)} %copy.189), kind=kOutput, calls=%fused_computation | convolution fusion | flops 422707200 | bytes 3932160 | tf_op jit(solution)/shard_map/sic,sjd->ijcd/dot_general | solution.py:169
  236.5 3.1 fusion.76
  239.6 0.5 multiply_reduce_fusion.1
  240.1 1.1 fusion.45
  241.2 2.0 copy-done.2
  243.2 1.2 fusion.32
  244.5 1.5 copy.159
  245.9 2.0 reshape.159
  248.0 17.8 %all_to_all.48 = bf16[16,2,6400]{2,1,0:T(2,128)(2,1)S(1)} all-to-all(bf16[16,2,6400]{2,1,0:T(2,128)(2,1)S(1)} %reshape.159), channel_id=1, replica_groups=mesh['row_0'=2,'row_1'=8,'col'=16] {'row_0','row_1'}, dimensions={0} | all-to-all | bytes 819200 | tf_op jit(solution)/shard_map/all_to_all | solution.py:193
  265.8 2.0 reshape.160
  267.8 1.6 copy.183
  269.4 3.6 reshape.161
  273.1 18.2 %all_to_all.49 = bf16[16,2,6400]{2,1,0:T(2,128)(2,1)S(1)} all-to-all(bf16[16,2,6400]{2,1,0:T(2,128)(2,1)S(1)} %reshape.161), channel_id=1, replica_groups=mesh['row_0'=2,'row_1'=8,'col'=16] {'col'}, dimensions={0} | all-to-all | bytes 819200 | tf_op jit(solution)/shard_map/all_to_all | solution.py:192
  291.2 2.0 reshape.162
  293.3 2.6 copy.210
  295.9 2.5 all_gather.31
  298.4 14.0 %all_gather.32 = bf16[2,40,640,8]{2,3,1,0:T(8,128)(2,1)} all-gather(bf16[1,40,640,8]{2,3,1,0:T(8,128)(2,1)S(1)} %all_gather.31), channel_id=1, replica_groups=mesh['row_0'=2,'row_1'=8,'col'=16] {'row_0'}, dimensions={0}, use_global_device_ids=true | all-gather | bytes 1228800 | tf_op jit(solution)/shard_map/all_gather | solution.py:40
  312.5 11.6 %copy.168 = bf16[40,640,128]{1,0,2:T(8,128)(2,1)} copy(bf16[40,640,128]{2,0,1:T(8,128)(2,1)} %all-gather.10.cloned.1.call-done) | data formatting | bytes 13107200 | tf_op jit(solution)/shard_map/all_gather | solution.py:200
  324.1 60.7 %all-gather.12.cloned.1.call-done = bf16[16,40,640,8]{2,3,1,0:T(8,128)(2,1)} async-done(((bf16[2,40,640,8]{2,3,1,0:T(8,128)(2,1)}), bf16[16,40,640,8]{2,3,1,0:T(8,128)(2,1)}) %all-gather.12.cloned.1.call-update) | async-done | bytes 6553616 | tf_op jit(solution)/shard_map/all_gather | solution.py:40
  384.8 6.4 %copy.164 = bf16[2,8,40,640,8]{3,4,2,1,0:T(8,128)(2,1)} copy(bf16[2,8,40,640,8]{3,4,2,0,1:T(8,128)(2,1)} %bitcast.108) | data formatting | bytes 13107200 | tf_op jit(solution)/shard_map/transpose | solution.py:43
  391.1 4.2 %copy.165 = bf16[40,640,16,8]{1,0,3,2:T(8,128)(2,1)S(1)} copy(bf16[40,640,16,8]{1,3,0,2:T(8,128)(2,1)} %bitcast.105) | data formatting | bytes 13107200 | tf_op jit(solution)/shard_map/transpose | solution.py:14
  395.4 2.3 bitcast_reduce_fusion
  397.8 0.4 multiply_reduce_fusion
  398.2 0.3 multiply_convert_fusion.1
  398.5 0.4 copy-done.12
  398.9 1.7 fusion.20
  400.6 0.8 copy.171
  (63 shorter events, 2.1 us)
Async XLA Ops:
  7.2 3.4 copy-start
  7.2 5.7 %copy-start.4 = (bf16[40,40,128]{2,1,0:T(8,128)(2,1)S(1)}, bf16[40,40,128]{2,1,0:T(8,128)(2,1)}, u32[]{:S(2)}) copy-start(bf16[40,40,128]{2,1,0:T(8,128)(2,1)} %param.10) | copy-start | bytes 1228804
  7.2 67.9 %all-gather.6.cloned.1.call-start = ((), (), s32[]{:S(2)}) async-start(), calls=%async_computation.4 | async-start | bytes 5570560 | tf_op jit(solution)/shard_map/all_gather | solution.py:30
  10.6 3.2 copy-start.13
  47.2 16.7 %all-to-all-start.1 = ((bf16[16,2,6400]{2,1,0:T(2,128)(2,1)}), bf16[16,2,6400]{2,1,0:T(2,128)(2,1)S(1)}, u32[]{:S(2)}, u32[]{:S(2)}) async-start(bf16[16,2,6400]{2,1,0:T(2,128)(2,1)} %reshape.157), calls=%async_computation.1 | async-start | bytes 819200 | tf_op jit(solution)/shard_map/all_to_all | solution.py:107
  53.0 174.6 %all-gather.8.cloned.1.call-start = ((), (), s32[]{:S(2)}) async-start(), calls=%async_computation.5 | async-start | bytes 5570560 | tf_op jit(solution)/shard_map/all_gather | solution.py:165
  86.5 3.5 copy-start.3
  90.0 1.7 copy-start.5
  93.3 2.0 copy-start.6
  93.3 2.0 copy-start.10
  93.3 2.7 copy-start.11
  95.6 74.6 %copy-start.7 = (bf16[8,40,256]{2,1,0:T(8,128)(2,1)}, bf16[8,40,256]{2,1,0:T(8,128)(2,1)S(1)}, u32[]{:S(2)}) copy-start(bf16[8,40,256]{2,1,0:T(8,128)(2,1)S(1)} %get-tuple-element.23) | copy-start | bytes 491524
  119.8 192.6 %all-gather.10.cloned.1.call-start = ((), (), s32[]{:S(2)}) async-start(), calls=%async_computation.6 | async-start | bytes 6963200 | tf_op jit(solution)/shard_map/all_gather | solution.py:200
  230.6 5.8 %copy-start.8 = (bf16[1024,128]{1,0:T(8,128)(2,1)S(1)}, bf16[1024,128]{1,0:T(8,128)(2,1)}, u32[]{:S(2)}) copy-start(bf16[1024,128]{1,0:T(8,128)(2,1)} %param.15) | copy-start | bytes 786436
  236.5 3.6 copy-start.9
  241.2 2.0 copy-start.2
  244.4 140.4 %all-gather.12.cloned.1.call-start = ((), (), s32[]{:S(2)}) async-start(), calls=%async_computation.7 | async-start | bytes 7372800 | tf_op jit(solution)/shard_map/all_gather | solution.py:40
  384.8 10.6 %slice-start = ((s8[6553600]{0:T(1024)(128)(4,1)}), s8[4194304]{0:T(1024)(128)(4,1)S(1)}, s32[]{:S(2)}) async-start(s8[6553600]{0:T(1024)(128)(4,1)} %bitcast.102), calls=%async_computation.8 | async-start | bytes 8388608
  391.1 4.3 %slice-start.1 = ((s8[6553600]{0:T(1024)(128)(4,1)}), s8[2359296]{0:T(1024)(128)(4,1)S(1)}, s32[]{:S(2)}) async-start(s8[6553600]{0:T(1024)(128)(4,1)} %bitcast.102), calls=%async_computation.9 | async-start | bytes 4718592
  398.2 0.8 copy-start.12
  398.2 3.2 copy-start.1
Sparse Core Ops, SparseCore 0:
  13.0 50.3 all-gather.5
  120.0 107.5 all-gather.7
  244.5 50.5 all-gather.9
  312.6 72.1 all-gather.11
where the time goes:
time: 417 us; the launch traced here: 408 us
  blocking collectives  147 us (35%)
  waiting for transfers between devices  126 us (30%)
  local copies, waits for them, and re-layouts  80.8 us (19%)
  matrix products  21.6 us (5%)
  between operations  14.6 us (4%)
  other arithmetic  11.4 us (3%)
  starting transfers between devices  6.46 us (2%)
    all_gather x1, waiting for transfers between devices, all_blocks(): blocks = lax.all_gather(blocks, axes[k])  60.7 us
    all_gather x1, waiting for transfers between devices, shards(): lax.all_gather(left_wide, ROW, axis=0, tiled=True)  57.4 us
    all_gather x1, blocking collectives, shards(): lax.all_gather(right_side, ROW, axis=0, tiled=True)  50.2 us
    all_to_all x1, blocking collectives, copy_for_each(): return lax.all_to_all(copies, axis, split_axis=0, concat_axis=0, tiled=True)  24.6 us
    unnamed x44, local copies, waits for them, and re-layouts  23.3 us
    all_gather x1, blocking collectives, shards(): left_wide = lax.all_gather(left_side, 'col', axis=1, tiled=True)  22.2 us
    all_to_all x1, blocking collectives, shards(): lax.all_to_all(lax.all_to_all(right_edge, ROW, split_axis=2, concat_axis=...  18.2 us
    all_to_all x1, blocking collectives, shards(): lax.all_to_all(right_edge, ROW, split_axis=2, concat_axis=0, tiled=True)  17.8 us
  transfers between devices with their start and end apart: 5, of which 3 were waited for; matrix products, arithmetic and copies ran while one was open for 12% of the time, Pallas kernels for 0%

commit v1 on v0

v1 whole, which is shorter than its diff:
```python
import functools

import jax
import jax.numpy as jnp
from jax import lax
from jax.experimental import pallas as pl
from jax.experimental.pallas import tpu as pltpu
from jax.sharding import PartitionSpec as P

MESH = pl.DeviceIdType.MESH
EPS = 1e-05
N = 16
BF = jnp.bfloat16
F32 = jnp.float32


def standardize(v, axis=-1):
    v = v.astype(F32)
    center = v - jnp.mean(v, axis=axis, keepdims=True)
    spread = jnp.mean(center * center, axis=axis, keepdims=True)
    return center * lax.rsqrt(spread + EPS)


def here():
    return lax.axis_index("row"), lax.axis_index("col")


def push(src, dst, send, recv, to):
    pltpu.make_async_remote_copy(src, dst, send, recv, device_id=to, device_id_type=MESH).start()


def local(src, dst, recv):
    pltpu.make_async_copy(src, dst, recv).start()


def drain(ref, sem):
    pltpu.make_async_copy(ref, ref, sem).wait()


def greet(to):
    pl.semaphore_signal(pltpu.get_barrier_semaphore(), inc=1, device_id=to, device_id_type=MESH)


def greeted(count):
    pl.semaphore_wait(pltpu.get_barrier_semaphore(), count)


def turned_greet(by_row):
    r, c = here()
    for s in range(N):
        k = lax.rem(c + s, N)
        to = (c, k) if by_row else (k, r)

        @pl.when((c != r) | (k != c))
        def _():
            greet(to)


def turned_push(src, dst, send, recv, by_row):
    r, c = here()
    slot = dst.at[c] if by_row else dst.at[r]
    for s in range(N):
        k = lax.rem(r + s, N)
        own = (k == r) & (r == c)
        to = (k, r) if by_row else (c, k)

        @pl.when(jnp.logical_not(own))
        def _():
            push(src, slot, send, recv, to)

        @pl.when(own)
        def _():
            local(src, slot, recv)


def turned_sent(dst, send):
    r, c = here()
    drain(dst.at[pl.ds(0, N - 1)], send)

    @pl.when(r != c)
    def _():
        drain(dst.at[0], send)


def comm_call(body, name, collective_id, outs, ins, sems, scratch=()):
    return pl.pallas_call(
        body,
        name=name,
        out_shape=outs,
        in_specs=[pl.BlockSpec(memory_space=pltpu.VMEM)] * len(ins),
        out_specs=jax.tree.map(lambda _: pl.BlockSpec(memory_space=pltpu.VMEM), outs),
        scratch_shapes=[pltpu.SemaphoreType.DMA((sems,)), *scratch],
        compiler_params=pltpu.CompilerParams(
            collective_id=collective_id, has_side_effects=True, vmem_limit_bytes=48 << 20
        ),
    )(*ins)


def entry_body(x, bias, xs, biases, sem):
    r, c = here()
    core = lax.rem(c, 2)
    mate = c + 1 - 2 * core
    for s in range(1, 8):
        greet((r, lax.rem(c + 2 * s, N)))
    greet((r, mate))
    turned_greet(True)
    greeted(8 + 15 + jnp.where(r == c, 0, 1))

    for s in range(1, 8):
        push(x, xs.at[c], sem.at[0], sem.at[2 + s], (r, lax.rem(c + 2 * s, N)))
    push(x, xs.at[c], sem.at[10], sem.at[2], (r, mate))
    local(x, xs.at[c], sem.at[11])
    turned_push(bias, biases, sem.at[12], sem.at[13], True)
    for s in range(1, 8):
        source = lax.rem(c - 2 * s + 2 * N, N)
        drain(xs.at[source], sem.at[2 + s])
        push(xs.at[source], xs.at[source], sem.at[10], sem.at[2], (r, mate))
    drain(xs.at[pl.ds(0, 7)], sem.at[0])
    drain(xs.at[pl.ds(0, 8)], sem.at[10])
    drain(xs.at[pl.ds(0, 8)], sem.at[2])
    drain(xs.at[0], sem.at[11])
    turned_sent(biases, sem.at[12])
    drain(biases, sem.at[13])


def sides_body(left, right, lefts, rights, sem):
    r, c = here()
    for s in range(1, N):
        greet((lax.rem(r + s, N), c))
    turned_greet(False)
    greeted(15 + 15 + jnp.where(r == c, 0, 1))

    turned_push(left, lefts, sem.at[0], sem.at[1], False)
    for s in range(1, N):
        push(right, rights.at[r], sem.at[2], sem.at[3], (lax.rem(r + s, N), c))
    local(right, rights.at[r], sem.at[3])
    turned_sent(lefts, sem.at[0])
    drain(lefts, sem.at[1])
    drain(rights.at[pl.ds(0, N - 1)], sem.at[2])
    drain(rights, sem.at[3])


def over_col_body(left, right, got, sem):
    r, c = here()
    side = lax.rem(r, 2)
    for s in range(1, N):
        greet((r, lax.rem(c + s, N)))
    greeted(15)
    for s in range(8):
        g = lax.rem(c // 2 + s, 8)
        for ref, to in ((left, 2 * g + 1 - side), (right, 2 * g + side)):
            if s == 0:

                @pl.when(to != c)
                def _():
                    push(ref.at[g], got.at[c], sem.at[0], sem.at[1], (r, to))

                @pl.when(to == c)
                def _():
                    local(ref.at[g], got.at[c], sem.at[1])
            else:
                push(ref.at[g], got.at[c], sem.at[0], sem.at[1], (r, to))
    drain(got.at[pl.ds(0, N - 1)], sem.at[0])
    drain(got, sem.at[1])


def over_row_body(parts, got, mates, sem):
    r, c = here()
    core = lax.rem(c, 2)
    mate = c + 1 - 2 * core
    kind = lax.rem(r + core, 2)
    for s in range(1, N):
        greet((lax.rem(r + s, N), c))
    greet((r, mate))
    greeted(16)
    for s in range(1, N):
        q = lax.rem(r + s, N)
        push(parts.at[q], got.at[kind, r // 2], sem.at[0], sem.at[1 + lax.rem(r, 2)], (q, c))
    local(parts.at[r], got.at[kind, r // 2], sem.at[1 + lax.rem(r, 2)])
    drain(got.at[1], sem.at[2 - core])
    push(got.at[1], mates, sem.at[3], sem.at[4], (r, mate))
    drain(parts.at[pl.ds(0, N - 1)], sem.at[0])
    drain(got.at[0], sem.at[1 + core])
    drain(mates, sem.at[3])
    drain(mates, sem.at[4])


def back_row_body(parts, got, sem):
    r, c = here()
    for s in range(1, N):
        greet((lax.rem(r + s, N), c))
    greeted(15)
    for s in range(1, N):
        q = lax.rem(r + s, N)
        push(parts.at[q], got.at[r], sem.at[0], sem.at[1], (q, c))
    local(parts.at[r], got.at[r], sem.at[1])
    drain(parts.at[pl.ds(0, N - 1)], sem.at[0])
    drain(got, sem.at[1])


def back_col_body(parts, got, sem):
    r, c = here()
    core = lax.rem(c, 2)
    mine = c // 2
    for s in range(1, 8):
        greet((r, lax.rem(c + 2 * s, N)))
    greeted(7)
    for s in range(1, 8):
        g = lax.rem(mine + s, 8)
        push(parts.at[g], got.at[mine], sem.at[0], sem.at[1], (r, 2 * g + core))
    local(parts.at[mine], got.at[mine], sem.at[1])
    drain(parts.at[pl.ds(0, 7)], sem.at[0])
    drain(got, sem.at[1])


def like(shape, dtype=BF):
    return jax.ShapeDtypeStruct(shape, dtype)


def shards(x, pair, w_in, w_out, w_bias, w_sides, w_outer, w_tri, w_tri_out):
    core = lax.rem(lax.axis_index("col"), 2)
    S, B, C = x.shape
    Z = pair.shape[2]
    H = w_bias.shape[1]
    D = C // H
    O = w_sides.shape[1] // 2
    SP = S * N
    R = B * N

    pair_n = standardize(pair).astype(BF).reshape(B * B, Z)
    bias = jnp.einsum("ch,pc->hp", w_bias, pair_n, preferred_element_type=F32).astype(BF)
    xs, biases = comm_call(
        entry_body, "entry_exchange", 1, [like((N, S, B, C)), like((N, H, B * B))], [x, bias], 14
    )
    biases = biases.reshape(N, H, B, B).transpose(1, 2, 0, 3).reshape(H, B, R)
    own_n = standardize(x).astype(BF).reshape(-1, C)
    all_n = standardize(xs).astype(BF).transpose(1, 0, 2, 3).reshape(-1, C)
    own = jnp.dot(own_n, jnp.concatenate([w_in[:, :C], w_in[:, 3 * C :]], 1), preferred_element_type=F32)
    kv = jnp.dot(all_n, w_in[:, C : 3 * C], preferred_element_type=F32).astype(BF)
    q = (own[:, :C] * D ** (-0.5)).astype(BF).reshape(S, B, H, D)
    gate = jax.nn.sigmoid(own[:, C:]).reshape(S, B, C)
    k = kv[:, :C].reshape(S, R, H, D)
    v = kv[:, C:].reshape(S, R, H, D)
    scores = jnp.einsum("sihd,sjhd->shij", q, k, preferred_element_type=F32) + biases.astype(F32)
    peak = jnp.max(scores, -1, keepdims=True)
    e = jnp.exp(scores - peak)
    total = jnp.sum(e, -1)
    att = jnp.einsum("shij,sjhd->sihd", e.astype(BF), v, preferred_element_type=F32)
    att = (att / jnp.transpose(total, (0, 2, 1))[..., None]).reshape(S, B, C)
    gated = (gate * att).astype(BF)
    x_new = (
        x.astype(F32)
        + jnp.dot(gated.reshape(-1, C), w_out, preferred_element_type=F32).reshape(S, B, C)
    ).astype(BF)
    sides = jnp.dot(
        standardize(x_new).astype(BF).reshape(-1, C), w_sides, preferred_element_type=F32
    ).astype(BF).reshape(S, B, 2 * O)
    left, right = sides[..., :O].reshape(S, B * O), sides[..., O:].reshape(S, B * O)
    lefts, rights = comm_call(
        sides_body, "sides_exchange", 2, [like((N, S, B * O))] * 2, [left, right], 4
    )
    lefts = lefts.reshape(SP, B, O)
    rights = rights.reshape(SP, B, O)
    products = jnp.einsum("sic,sjd->ijcd", lefts, rights, preferred_element_type=F32)
    averaged = (products * (1.0 / SP)).astype(BF).reshape(B * B, O * O)
    pair_mid = (
        pair.astype(F32) + jnp.dot(averaged, w_outer, preferred_element_type=F32).reshape(B, B, Z)
    ).astype(BF)
    tri_n = standardize(pair_mid).astype(BF).reshape(B * B, Z)
    edges = jnp.einsum("cn,pc->np", w_tri[:, : 4 * Z], tri_n, preferred_element_type=F32)
    left_edge = (jax.nn.sigmoid(edges[Z : 2 * Z]) * edges[:Z]).astype(BF)
    right_edge = (jax.nn.sigmoid(edges[3 * Z :]) * edges[2 * Z : 3 * Z]).astype(BF)
    out_gate = jax.nn.sigmoid(jnp.dot(tri_n, w_tri[:, 4 * Z :], preferred_element_type=F32))
    got = comm_call(
        over_col_body, "edges_over_col", 3, like((N, N, B * B)),
        [left_edge.reshape(8, N, B * B), right_edge.reshape(8, N, B * B)], 2,
    )
    parts = got.reshape(N, N, B, B).transpose(1, 2, 0, 3).reshape(N, B, R)
    got, mates = comm_call(
        over_row_body, "edges_over_row", 4, [like((2, 8, B, R)), like((8, B, R))], [parts], 5
    )
    r_all = got[0].reshape(8 * B, R)
    l_other = jnp.dot(got[1].reshape(8 * B, R), r_all.T, preferred_element_type=F32).astype(BF)
    l_same = jnp.dot(mates.reshape(8 * B, R), r_all.T, preferred_element_type=F32).astype(BF)
    l_other, l_same = l_other.reshape(8, B, 8 * B), l_same.reshape(8, B, 8 * B)
    even = jnp.where(core == 0, l_same, l_other)
    odd = jnp.where(core == 0, l_other, l_same)
    sums = jnp.stack([even, odd], 1).reshape(N, B, 8 * B)
    got = comm_call(back_row_body, "sums_over_row", 5, like(sums.shape), [sums], 2)
    parts = got.reshape(N, B, 8, B).transpose(2, 0, 1, 3).reshape(8, N, B * B)
    got = comm_call(back_col_body, "sums_over_col", 6, like(parts.shape), [parts], 2)
    tri_ln = standardize(got.reshape(Z, B * B), 0).astype(BF)
    update = jnp.einsum("cp,cn->pn", tri_ln, w_tri_out, preferred_element_type=F32)
    pair_new = (pair_mid.astype(F32) + (out_gate * update).reshape(B, B, Z)).astype(BF)
    return x_new, pair_new


def solution(mesh):
    tile = P("row", "col", None)
    return jax.shard_map(
        shards,
        mesh=mesh,
        in_specs=(tile, tile) + (P(),) * 7,
        out_specs=(tile, tile),
        check_vma=False,
    )
```

time: 417 us -> 251 us (0.60); the launches traced: 408 us -> 247 us
  blocking collectives: 147 us -> 0 us
  Pallas kernels: 0 us -> 145 us
  waiting for transfers between devices: 126 us -> 0 us
  local copies, waits for them, and re-layouts: 80.8 us -> 54.9 us
  between operations: 14.6 us -> 1.48 us
  matrix products: 21.6 us -> 31.1 us
  starting transfers between devices: 6.46 us -> 0 us
    pallas_call x0 -> x6, Pallas kernels: none -> 145 us  [comm_call(): pl.pallas_call(body, name=name, out_shape=outs, in_specs=[pl.BlockSpec(me...]
    all_gather x4 -> x0, waiting for transfers between devices: 118 us -> none  [the longest x1 60.7 us: all_blocks(): blocks = lax.all_gather(blocks, axes[k])]
    all_gather x3 -> x0, blocking collectives: 86.4 us -> none  [the longest x1 50.2 us: shards(): lax.all_gather(right_side, ROW, axis=0, tiled=True)]
    all_to_all x3 -> x0, blocking collectives: 60.5 us -> none  [the longest x1 24.6 us: copy_for_each(): return lax.all_to_all(copies, axis, split_axis=0, concat_axis=0, tiled=True)]
    reshape x4 -> x14, local copies, waits for them, and re-layouts: 2.91 us -> 25 us  [the longest x3 12.9 us: shards(): parts = got.reshape(N, N, B, B).transpose(1, 2, 0, 3).reshape(N, B, R)]
    all_gather x3 -> x0, local copies, waits for them, and re-layouts: 15.4 us -> none  [the longest x1 11.6 us: shards(): arrived = lax.all_gather(left_edge, 'col', axis=1, tiled=True)]
    unnamed x44 -> x32, local copies, waits for them, and re-layouts: 23.3 us -> 9.53 us
    transpose x3 -> x1, local copies, waits for them, and re-layouts: 10.7 us -> 0.17 us  [shards(): all_n = standardize(xs).astype(BF).transpose(1, 0, 2, 3).reshape(-1, C)]
  transfers between devices with their start and end apart: 5 -> 0, of which waited for: 3 -> 0; matrix products, arithmetic and copies ran while one was open for 12% -> 0% of each run, Pallas kernels for 0% -> 0%
where the time goes in v1:
time: 251 us; the launch traced here: 247 us
  Pallas kernels  145 us (58%)
  local copies, waits for them, and re-layouts  54.9 us (22%)
  matrix products  31.1 us (12%)
  other arithmetic  14.3 us (6%)
    pallas_call x6, Pallas kernels, comm_call(): pl.pallas_call(body, name=name, out_shape=outs, in_specs=[pl.BlockSpec(me...  145 us
    dot_general x1, matrix products, shards(): jnp.einsum('shij,sjhd->sihd', e.astype(BF), v, preferred_element_type=F32)  13.5 us
    reshape x3, local copies, waits for them, and re-layouts, shards(): parts = got.reshape(N, N, B, B).transpose(1, 2, 0, 3).reshape(N, B, R)  12.9 us
    convert_element_type x3, local copies, waits for them, and re-layouts, shards(): biases.astype(F32)  10.8 us
    unnamed x32, local copies, waits for them, and re-layouts  9.53 us
    reshape x3, local copies, waits for them, and re-layouts, shards(): parts = got.reshape(N, B, 8, B).transpose(2, 0, 1, 3).reshape(8, N, B * B)  6.91 us
    dot_general x1, matrix products, shards(): jnp.einsum('sic,sjd->ijcd', lefts, rights, preferred_element_type=F32)  5.86 us

profile of v1, /device:TPU:8, one launch (start us, length us, event | category | flops | bytes accessed | tf_op | source)
XLA Modules:
  0.0 247.2 jit_solution(12624974218998779352)
XLA Ops:
  0.6 1.3 convert_reduce_fusion.2
  2.0 1.5 fusion.38
  3.5 1.5 fusion.39
  5.0 0.9 fusion.17.bias
  5.9 0.9 copy-done.1
  6.9 40.3 %entry_exchange.1 = (bf16[16,8,40,256]{3,2,1,0:T(8,128)(2,1)S(1)}, bf16[16,8,1600]{2,1,0:T(8,128)(2,1)S(1)}) custom-call(bf16[8,40,256]{2,1,0:T(8,128)(2,1)S(1)} %copy-done.1, bf16[8,1600]{1,0:T(8,128)(2,1)S(1)} %fusion.17.bias), custom_call_target="tpu_custom_call" | custom-call | tf_op jit(solution)/shard_map/entry_exchange/pallas_call | solution.py:86
  47.1 0.7 convert_reduce_fusion
  47.9 1.9 fusion.4
  49.9 1.7 fusion.10
  51.6 0.2 copy.26
  51.8 0.9 copy-done.11
  52.6 1.5 convolution_convert_fusion
  54.1 1.9 fusion.78
  56.0 2.8 %copy.29 = bf16[5120,256]{0,1:T(8,128)(2,1)} copy(bf16[5120,256]{1,0:T(8,128)(2,1)S(1)} %get-tuple-element.17) | data formatting | bytes 5242880 | tf_op jit(solution)/shard_map/slice | solution.py:242
  58.9 2.2 copy.56
  61.1 2.6 %reshape.240 = f32[16,8,40,40]{3,2,1,0:T(8,128)} reshape(bf16[16,8,1600]{2,1,0:T(8,128)(2,1)S(1)} %get-tuple-element.9) | data formatting | bytes 1228800 | tf_op jit(solution)/shard_map/convert_element_type | solution.py:244
  63.7 4.8 %copy.79 = f32[16,8,40,40]{3,0,2,1:T(8,128)} copy(f32[16,8,40,40]{3,2,1,0:T(8,128)} %reshape.240) | data formatting | bytes 1638400 | tf_op jit(solution)/shard_map/convert_element_type | solution.py:244
  68.5 3.4 %reshape.238 = f32[8,40,640]{2,1,0:T(8,128)} reshape(f32[8,40,16,40]{3,2,1,0:T(8,128)} %bitcast.103) | data formatting | bytes 1638400 | tf_op jit(solution)/shard_map/convert_element_type | solution.py:244
  72.0 0.2 fusion.55
  72.4 1.0 fusion.80
  73.4 0.2 fusion.66
  73.7 0.8 copy-done.8
  74.5 1.1 reshape.245
  75.6 2.7 %add_reduce_fusion = (f32[8,8,40]{2,1,0:T(8,128)S(1)}, f32[8,8,40,640]{3,2,1,0:T(8,128)S(1)}) fusion(f32[8,40,640]{2,1,0:T(8,128)} %reshape.238, bf16[8,640,8,32]{1,0,3,2:T(8,128)(2,1)S(1)} %bitcast.100, bf16[8,40,8,32]{3,2,1,0:T(8,128)(2,1)} %reshape.245), kind=kOutput, calls=%fused_computation.7 | convolution fusion | flops 108131840 | bytes 10168320 | tf_op jit(solution)/shard_map/sihd,sjhd->shij/dot_general | solution.py:244
  78.4 1.6 fusion.2
  79.9 1.5 copy-done.3
  81.5 0.6 copy-done.6
  82.1 2.9 %copy.27 = bf16[5120,256]{0,1:T(8,128)(2,1)} copy(bf16[5120,256]{1,0:T(8,128)(2,1)S(1)} %copy-done.6) | data formatting | bytes 5242880 | tf_op jit(solution)/shard_map/slice | solution.py:243
  84.9 2.3 copy.55
  87.3 13.5 %fusion.29 = f32[8,40,8,32]{1,3,2,0:T(8,128)S(1)} fusion(f32[8,8,40,640]{3,2,1,0:T(8,128)} %copy-done.3, f32[8,8,40]{2,1,0:T(8,128)S(1)} %get-tuple-element.28, f32[8,40,640]{2,1,0:T(8,128)S(1)} %copy-done.5, bf16[8,640,8,32]{1,0,3,2:T(8,128)(2,1)S(1)} %bitcast.109, f32[8,40,8]{1,2,0:T(8,128)S(1)} %bitcast.122), kind=kOutput, calls=%fused_computation.47 | convolution fusion | flops 109854720 | bytes 10342400 | tf_op jit(solution)/shard_map/shij,sjhd->sihd/dot_general | solution.py:248
  100.8 0.5 copy.51
  101.3 0.4 reshape.246
  101.7 0.2 copy-done.9
  102.0 1.2 convert_reduce_fusion.5
  103.2 0.2 fusion.57
  103.6 0.2 convolution_convert_fusion.4
  104.3 32.7 %sides_exchange.1 = (bf16[16,8,1280]{2,1,0:T(8,128)(2,1)S(1)}, bf16[16,8,1280]{2,1,0:T(8,128)(2,1)S(1)}) custom-call(bf16[8,1280]{1,0:T(8,128)(2,1)S(1)} %reshape.224.left, bf16[8,1280]{1,0:T(8,128)(2,1)S(1)} %reshape.225.right), custom_call_target="tpu_custom_call" | custom-call | tf_op jit(solution)/shard_map/sides_exchange/pallas_call | solution.py:86
  136.9 0.9 reshape.227
  137.8 1.2 copy.38
  139.1 0.9 reshape.226
  140.0 5.9 %multiply_convert_fusion = bf16[40,32,40,32]{2,1,3,0:T(8,128)(2,1)S(1)} fusion(bf16[128,40,32,1]{2,1,0,3:T(8,128)(2,1)S(1)} %bitcast.106, bf16[128,40,32]{0,1,2:T(8,128)(2,1)S(1)} %copy.38), kind=kOutput, calls=%fused_computation | convolution fusion | flops 422707200 | bytes 3932160 | tf_op jit(solution)/shard_map/sic,sjd->ijcd/dot_general | solution.py:264
  145.9 2.9 %fusion.70 = f32[40,40,128]{2,0,1:T(8,128)S(1)} fusion(bf16[40,40,1024]{0,2,1:T(8,128)(2,1)S(1)} %bitcast.99, bf16[1024,128]{1,0:T(8,128)(2,1)S(1)} %copy-done), kind=kOutput, calls=%fused_computation.98 | convolution fusion | flops 419430400 | bytes 4358144 | tf_op jit(solution)/shard_map/dot_general | solution.py:267
  148.8 0.3 convert_reduce_fusion.1
  149.2 0.5 fusion.36
  149.7 0.5 fusion.37
  150.2 0.6 convolution_bitcast_fusion
  150.8 0.4 fusion.42
  151.2 0.3 copy.40
  151.5 0.3 copy.41
  151.7 19.2 %edges_over_col.1 = bf16[16,16,1600]{2,1,0:T(8,128)(2,1)S(1)} custom-call(bf16[8,16,1600]{2,1,0:T(8,128)(2,1)S(1)} %bitcast.96, bf16[8,16,1600]{2,1,0:T(8,128)(2,1)S(1)} %bitcast.97), custom_call_target="tpu_custom_call" | custom-call | tf_op jit(solution)/shard_map/edges_over_col/pallas_call | solution.py:86
  170.9 3.6 %reshape.231 = bf16[16,16,40,40]{3,2,1,0:T(8,128)(2,1)} reshape(bf16[16,16,1600]{2,1,0:T(8,128)(2,1)S(1)} %edges_over_col.1) | data formatting | bytes 1638400 | tf_op jit(solution)/shard_map/reshape | solution.py:278
  174.6 5.0 %copy.78 = bf16[16,16,40,40]{3,0,2,1:T(8,128)(2,1)} copy(bf16[16,16,40,40]{3,2,1,0:T(8,128)(2,1)} %reshape.231) | data formatting | bytes 1638400 | tf_op jit(solution)/shard_map/reshape | solution.py:278
  179.5 4.3 %reshape.232.parts = bf16[16,40,640]{2,1,0:T(8,128)(2,1)S(1)} reshape(bf16[16,40,16,40]{3,2,1,0:T(8,128)(2,1)} %bitcast.105) | data formatting | bytes 1638400 | tf_op jit(solution)/shard_map/reshape | solution.py:278
  183.8 26.1 %edges_over_row.1 = (bf16[2,8,40,640]{3,2,1,0:T(8,128)(2,1)S(1)}, bf16[8,40,640]{2,1,0:T(8,128)(2,1)S(1)}) custom-call(bf16[16,40,640]{2,1,0:T(8,128)(2,1)S(1)} %reshape.232.parts), custom_call_target="tpu_custom_call" | custom-call | tf_op jit(solution)/shard_map/edges_over_row/pallas_call | solution.py:86
  210.0 0.4 convolution_convert_fusion.2
  210.4 0.4 broadcast_select_fusion.1
  210.9 18.2 %sums_over_row.1 = bf16[16,40,320]{2,1,0:T(8,128)(2,1)S(1)} custom-call(bf16[16,40,320]{2,1,0:T(8,128)(2,1)S(1)} %bitcast.95), custom_call_target="tpu_custom_call" | custom-call | tf_op jit(solution)/shard_map/sums_over_row/pallas_call | solution.py:86
  229.1 2.2 reshape.235
  231.3 2.6 %copy.80 = bf16[16,40,8,40]{3,1,0,2:T(8,128)(2,1)} copy(bf16[16,40,8,40]{3,2,1,0:T(8,128)(2,1)} %reshape.235) | data formatting | bytes 819200 | tf_op jit(solution)/shard_map/reshape | solution.py:290
  233.8 2.2 reshape.236.parts
  236.1 9.1 %sums_over_col.1 = bf16[8,16,1600]{2,1,0:T(8,128)(2,1)S(1)} custom-call(bf16[8,16,1600]{2,1,0:T(8,128)(2,1)S(1)} %reshape.236.parts), custom_call_target="tpu_custom_call" | custom-call | tf_op jit(solution)/shard_map/sums_over_col/pallas_call | solution.py:86
  245.5 0.4 fusion.16
  245.9 0.3 convolution_multiply_fusion
  246.2 0.8 fusion.41
  (50 shorter events, 1.6 us)
Async XLA Ops:
  0.6 145.2 %copy-start = (bf16[1024,128]{1,0:T(8,128)(2,1)S(1)}, bf16[1024,128]{1,0:T(8,128)(2,1)}, u32[]{:S(2)}) copy-start(bf16[1024,128]{1,0:T(8,128)(2,1)} %param.15) | copy-start | bytes 786436
  5.9 0.9 copy-start.1
  51.6 1.0 copy-start.11
  63.7 8.2 %copy-start.2 = (bf16[8,40,256]{2,1,0:T(8,128)(2,1)S(1)}, bf16[8,40,256]{2,1,0:T(8,128)(2,1)}, u32[]{:S(2)}) copy-start(bf16[8,40,256]{2,1,0:T(8,128)(2,1)} %x.1) | copy-start | bytes 491524
  73.7 0.8 copy-start.8
  75.6 2.7 %copy-start.4 = (f32[8,40,640]{2,1,0:T(8,128)S(1)}, f32[8,40,640]{2,1,0:T(8,128)}, u32[]{:S(2)}) copy-start(f32[8,40,640]{2,1,0:T(8,128)} %reshape.238) | copy-start | bytes 2457604
  78.3 3.1 %copy-start.3 = (f32[8,8,40,640]{3,2,1,0:T(8,128)}, f32[8,8,40,640]{3,2,1,0:T(8,128)S(1)}, u32[]{:S(2)}) copy-start(f32[8,8,40,640]{3,2,1,0:T(8,128)S(1)} %get-tuple-element.29) | copy-start | bytes 19660804
  78.4 3.7 %copy-start.6 = (bf16[5120,256]{1,0:T(8,128)(2,1)S(1)}, bf16[5120,256]{1,0:T(8,128)(2,1)}, u32[]{:S(2)}) copy-start(bf16[5120,256]{1,0:T(8,128)(2,1)} %get-tuple-element.16) | copy-start | bytes 7864324
  84.9 2.3 copy-start.5
  100.8 1.1 copy-start.9
  100.8 2.8 %copy-start.14 = (bf16[256,64]{0,1:T(8,128)(2,1)S(1)}, bf16[256,64]{0,1:T(8,128)(2,1)}, u32[]{:S(2)}) copy-start(bf16[256,64]{0,1:T(8,128)(2,1)} %param.14) | copy-start | bytes 98308
  103.2 42.7 %copy-start.10 = (bf16[8,40,256]{2,1,0:T(8,128)(2,1)}, bf16[8,40,256]{2,1,0:T(8,128)(2,1)S(1)}, u32[]{:S(2)}) copy-start(bf16[8,40,256]{2,1,0:T(8,128)(2,1)S(1)} %get-tuple-element.31) | copy-start | bytes 491524
  145.9 2.9 %copy-start.7 = (bf16[40,40,128]{2,1,0:T(8,128)(2,1)S(1)}, bf16[40,40,128]{2,1,0:T(8,128)(2,1)}, u32[]{:S(2)}) copy-start(bf16[40,40,128]{2,1,0:T(8,128)(2,1)} %param.10) | copy-start | bytes 1228804
  145.9 4.3 %copy-start.12 = (bf16[128,640]{1,0:T(8,128)(2,1)S(1)}, bf16[128,640]{1,0:T(8,128)(2,1)}, u32[]{:S(2)}) copy-start(bf16[128,640]{1,0:T(8,128)(2,1)} %param.16) | copy-start | bytes 491524
  236.0 9.8 %copy-start.13 = (bf16[128,128]{1,0:T(8,128)(2,1)S(1)}, bf16[128,128]{1,0:T(8,128)(2,1)}, u32[]{:S(2)}) copy-start(bf16[128,128]{1,0:T(8,128)(2,1)} %param.17) | copy-start | bytes 98308

commit v2 on v1

v2 whole, which is shorter than its diff:
```python
import functools

import jax
import jax.numpy as jnp
from jax import lax
from jax.experimental import pallas as pl
from jax.experimental.pallas import tpu as pltpu
from jax.sharding import PartitionSpec as P

MESH = pl.DeviceIdType.MESH
EPS = 1e-05
N = 16
BF = jnp.bfloat16
F32 = jnp.float32


def standardize(v, axis=-1):
    v = v.astype(F32)
    center = v - jnp.mean(v, axis=axis, keepdims=True)
    spread = jnp.mean(center * center, axis=axis, keepdims=True)
    return center * lax.rsqrt(spread + EPS)


def here():
    return lax.axis_index("row"), lax.axis_index("col")


def push(src, dst, send, recv, to):
    pltpu.make_async_remote_copy(src, dst, send, recv, device_id=to, device_id_type=MESH).start()


def local(src, dst, recv):
    pltpu.make_async_copy(src, dst, recv).start()


def drain(ref, sem):
    pltpu.make_async_copy(ref, ref, sem).wait()


def greet(to):
    pl.semaphore_signal(pltpu.get_barrier_semaphore(), inc=1, device_id=to, device_id_type=MESH)


def greeted(count):
    pl.semaphore_wait(pltpu.get_barrier_semaphore(), count)


def turned_greet(by_row):
    r, c = here()
    for s in range(N):
        k = lax.rem(c + s, N)
        to = (c, k) if by_row else (k, r)

        @pl.when((c != r) | (k != c))
        def _():
            greet(to)


def turned_push(src, dst, send, recv, by_row):
    r, c = here()
    slot = dst.at[c] if by_row else dst.at[r]
    for s in range(N):
        k = lax.rem(r + s, N)
        own = (k == r) & (r == c)
        to = (k, r) if by_row else (c, k)

        @pl.when(jnp.logical_not(own))
        def _():
            push(src, slot, send, recv, to)

        @pl.when(own)
        def _():
            local(src, slot, recv)


def turned_sent(dst, send):
    r, c = here()
    drain(dst.at[pl.ds(0, N - 1)], send)

    @pl.when(r != c)
    def _():
        drain(dst.at[0], send)


def comm_call(body, name, collective_id, outs, ins, sems, scratch=()):
    return pl.pallas_call(
        body,
        name=name,
        out_shape=outs,
        in_specs=[pl.BlockSpec(memory_space=pltpu.VMEM)] * len(ins),
        out_specs=jax.tree.map(lambda _: pl.BlockSpec(memory_space=pltpu.VMEM), outs),
        scratch_shapes=[*scratch, pltpu.SemaphoreType.DMA((sems,))],
        compiler_params=pltpu.CompilerParams(
            collective_id=collective_id, has_side_effects=True, vmem_limit_bytes=48 << 20
        ),
    )(*ins)


def attention_body(
    x, pair, w_in, w_out, w_bias, x_new, xs, bias_out, biases, bias, q_all, gates, sem
):
    r, c = here()
    core = lax.rem(c, 2)
    mate = c + 1 - 2 * core
    S, B, C = x.shape
    H = w_bias.shape[1]
    D = C // H
    for s in range(1, 8):
        greet((r, lax.rem(c + 2 * s, N)))
    greet((r, mate))
    turned_greet(True)
    greeted(8 + 15 + jnp.where(r == c, 0, 1))
    for s in range(1, 8):
        push(x, xs.at[c], sem.at[0], sem.at[2 + s], (r, lax.rem(c + 2 * s, N)))
    push(x, xs.at[c], sem.at[10], sem.at[2], (r, mate))
    local(x, xs.at[c], sem.at[11])
    pair_n = standardize(pair[...]).astype(BF).reshape(B * B, pair.shape[2])
    bias_out[...] = lax.dot_general(
        w_bias[...], pair_n, (((0,), (1,)), ((), ())), preferred_element_type=F32
    ).astype(BF)
    turned_push(bias_out, biases, sem.at[12], sem.at[13], True)
    own_n = standardize(x[...]).astype(BF).reshape(S * B, C)
    q = jnp.dot(own_n, w_in[:, :C], preferred_element_type=F32) * D ** (-0.5)
    q_all[...] = q.reshape(S, B, C)
    gates[...] = jax.nn.sigmoid(
        jnp.dot(own_n, w_in[:, 3 * C :], preferred_element_type=F32)
    ).reshape(S, B, C)
    for s in range(1, 8):
        source = lax.rem(c - 2 * s + 2 * N, N)
        drain(xs.at[source], sem.at[2 + s])
        push(xs.at[source], xs.at[source], sem.at[10], sem.at[2], (r, mate))
    turned_sent(biases, sem.at[12])
    drain(biases, sem.at[13])
    spread(lambda k: biases[k].astype(F32), bias, B)
    drain(xs.at[pl.ds(0, 7)], sem.at[0])
    drain(xs.at[pl.ds(0, 8)], sem.at[10])
    drain(xs.at[pl.ds(0, 8)], sem.at[2])
    drain(xs.at[0], sem.at[11])
    head = lax.broadcasted_iota(jnp.int32, (B, C), 1) // D

    @pl.loop(0, S)
    def _(s):
        x_s = standardize(xs[:, s]).reshape(N * B, C).astype(BF)
        k = jnp.dot(x_s, w_in[:, C : 2 * C], preferred_element_type=F32).astype(BF)
        v = jnp.dot(x_s, w_in[:, 2 * C : 3 * C], preferred_element_type=F32).astype(BF)
        q_s = q_all[s]
        q_h = jnp.concatenate([jnp.where(head == h, q_s, 0.0) for h in range(H)], 0).astype(BF)
        scores = lax.dot_general(
            q_h, k, (((1,), (1,)), ((), ())), preferred_element_type=F32
        ) + bias[...].reshape(H * B, N * B)
        e = jnp.exp(scores - jnp.max(scores, -1, keepdims=True))
        att = jnp.dot(e.astype(BF), v, preferred_element_type=F32)
        att = (att / jnp.sum(e, -1, keepdims=True)).reshape(H, B, C)
        total = jnp.where(head == 0, att[0], 0.0)
        for h in range(1, H):
            total = jnp.where(head == h, att[h], total)
        gated = (gates[s] * total).astype(BF)
        x_new[s] = (
            x[s].astype(F32) + jnp.dot(gated, w_out[...], preferred_element_type=F32)
        ).astype(BF)


def spread(block, out, B):
    blocks = [block(k) for k in range(N)]
    for i in range(B):
        out[:, i, :] = jnp.concatenate([b[:, i * B : (i + 1) * B] for b in blocks], 1)


def outer_body(
    x_new, pair, w_sides, w_outer, w_tri, got, mid, gate,
    by_residue, left, right, lefts, rights, tall, stacked, w_wide, normed, left_edge, right_edge, sem,
):
    r, c = here()
    S, B, C = x_new.shape
    O = w_sides.shape[1] // 2
    Z = pair.shape[2]
    for s in range(1, N):
        greet((lax.rem(r + s, N), c))
    turned_greet(False)
    for s in range(1, N):
        greet((r, lax.rem(c + s, N)))
    sides = jnp.dot(
        standardize(x_new[...]).astype(BF).reshape(S * B, C), w_sides[...], preferred_element_type=F32
    )
    for s in range(S):
        by_residue[:, s, : 2 * O] = sides[s * B : (s + 1) * B]
    left[...] = jnp.concatenate([by_residue[i, :, :O] for i in range(B)], 1).astype(BF)
    right[...] = jnp.concatenate([by_residue[i, :, O : 2 * O] for i in range(B)], 1).astype(BF)
    greeted(45 + jnp.where(r == c, 0, 1))
    turned_push(left, lefts, sem.at[0], sem.at[1], False)
    for s in range(1, N):
        push(right, rights.at[r], sem.at[2], sem.at[3], (lax.rem(r + s, N), c))
    local(right, rights.at[r], sem.at[3])

    w_wide[...] = jnp.zeros_like(w_wide)
    tall[pl.ds(0, O * O), :] = w_outer[...].astype(F32)
    for d in range(O):
        part = tall[pl.ds(d, O, stride=O), :].astype(BF)
        for i in range(4):
            w_wide[pl.ds(d * 4 * O + i * O, O), i * Z : (i + 1) * Z] = part
    turned_sent(lefts, sem.at[0])
    drain(lefts, sem.at[1])
    drain(rights.at[pl.ds(0, N - 1)], sem.at[2])
    drain(rights, sem.at[3])

    tall[...] = rights[...].reshape(S * N, B * O).astype(F32).T
    right_t = jnp.concatenate([tall[pl.ds(d, B, stride=O), :] for d in range(O)], 0).astype(BF)
    left_s = lefts[...].reshape(S * N, B * O)
    for g in range(B // 8):
        halves = [
            jnp.dot(
                right_t, left_s[:, k * 4 * O : (k + 1) * 4 * O], preferred_element_type=F32
            ) * (1.0 / (S * N))
            for k in (2 * g, 2 * g + 1)
        ]
        for d in range(O):
            stacked[pl.ds(g * 2 * B, 2 * B), d * 4 * O : (d + 1) * 4 * O] = jnp.concatenate(
                [h[d * B : (d + 1) * B] for h in halves], 0
            ).astype(BF)
    wide = jnp.dot(stacked[...], w_wide[...], preferred_element_type=F32)
    for i in range(B):
        k, u = i // 4, i % 4
        row = (pair[i].astype(F32) + wide[k * B : (k + 1) * B, u * Z : (u + 1) * Z]).astype(BF)
        mid[i] = row
        normed[pl.ds(i * B, B), :] = standardize(row)
    tri_n = normed[...].astype(BF)

    def edge(k):
        w = w_tri[:, 2 * k * Z : 2 * (k + 1) * Z]
        both = lax.dot_general(w, tri_n, (((0,), (1,)), ((), ())), preferred_element_type=F32)
        return (jax.nn.sigmoid(both[Z:]) * both[:Z]).astype(BF).reshape(8, N, B * B)

    parity = lax.rem(r, 2)
    for k, ref in ((0, left_edge), (1, right_edge)):
        ref[...] = edge(k)
        for s in range(8):
            g = lax.rem(c // 2 + s, 8)
            to = 2 * g + lax.rem(parity + 1 + k, 2)
            if s == 0:

                @pl.when(to != c)
                def _():
                    push(ref.at[g], got.at[c], sem.at[4], sem.at[5], (r, to))

                @pl.when(to == c)
                def _():
                    local(ref.at[g], got.at[c], sem.at[5])
            else:
                push(ref.at[g], got.at[c], sem.at[4], sem.at[5], (r, to))
    gate[...] = jax.nn.sigmoid(jnp.dot(tri_n, w_tri[:, 4 * Z :], preferred_element_type=F32))
    drain(got.at[pl.ds(0, N - 1)], sem.at[4])
    drain(got, sem.at[5])


def triangle_body(
    edges, mid, gate, w, out, spreads, parts, got, mates, sums, channel, back, flat, tiles, sem
):
    r, c = here()
    core = lax.rem(c, 2)
    mate = c + 1 - 2 * core
    mine = c // 2
    B = mid.shape[0]
    Z = mid.shape[2]
    R = N * B
    kind = lax.rem(r + core, 2)
    for s in range(1, N):
        greet((lax.rem(r + s, N), c))
    greet((r, mate))
    for s in range(1, 8):
        greet((r, lax.rem(c + 2 * s, N)))
    for h in range(2):
        spread(lambda k: edges[k].astype(F32)[8 * h : 8 * h + 8], spreads, B)
        parts[pl.ds(8 * h, 8)] = spreads[...].astype(BF)
        if h == 0:
            greeted(23)
        arrived = sem.at[1 + lax.rem(r, 2)]
        for s in range(8):
            q = 8 * h + lax.rem(r + s, 8)
            if s == 0:

                @pl.when(q != r)
                def _():
                    push(parts.at[q], got.at[kind, r // 2], sem.at[0], arrived, (q, c))

                @pl.when(q == r)
                def _():
                    local(parts.at[q], got.at[kind, r // 2], arrived)
            else:
                push(parts.at[q], got.at[kind, r // 2], sem.at[0], arrived, (q, c))
    drain(got.at[1], sem.at[2 - core])
    push(got.at[1], mates, sem.at[3], sem.at[4], (r, mate))
    drain(got.at[0], sem.at[1 + core])
    columns = got[0].reshape(8 * B, R)
    for rows, parity in ((got.at[1], 1 - core), (mates, core)):
        if rows is mates:
            drain(mates, sem.at[4])
        total = lax.dot_general(
            rows[...].reshape(8 * B, R), columns, (((1,), (1,)), ((), ())), preferred_element_type=F32
        )
        for s in range(8):
            q = 2 * s + parity
            sums[q] = total[s * B : (s + 1) * B].astype(BF)

            @pl.when(q != r)
            def _():
                push(sums.at[q], channel.at[r], sem.at[5], sem.at[6], (q, c))

            @pl.when(q == r)
            def _():
                local(sums.at[q], channel.at[r], sem.at[6])
    drain(parts.at[pl.ds(0, N - 1)], sem.at[0])
    drain(mates, sem.at[3])
    drain(sums.at[pl.ds(0, N - 1)], sem.at[5])
    drain(channel, sem.at[6])
    back[...] = channel[...].astype(F32)
    rows = [back[:, i, :] for i in range(B)]
    for g in range(8):
        flat[g] = jnp.concatenate([v[:, g * B : (g + 1) * B] for v in rows], 1).astype(BF)
    for s in range(1, 8):
        g = lax.rem(mine + s, 8)
        push(flat.at[g], tiles.at[mine], sem.at[7], sem.at[8], (r, 2 * g + core))
    local(flat.at[mine], tiles.at[mine], sem.at[8])
    drain(flat.at[pl.ds(0, 7)], sem.at[7])
    drain(tiles, sem.at[8])
    tri_ln = standardize(tiles[...].reshape(Z, B * B), 0).astype(BF)
    update = lax.dot_general(
        tri_ln, w[...], (((0,), (0,)), ((), ())), preferred_element_type=F32
    )
    out[...] = (mid[...].astype(F32) + (gate[...] * update).reshape(B, B, Z)).astype(BF)


def like(shape, dtype=BF):
    return jax.ShapeDtypeStruct(shape, dtype)


def shards(x, pair, w_in, w_out, w_bias, w_sides, w_outer, w_tri, w_tri_out):
    core = lax.rem(lax.axis_index("col"), 2)
    S, B, C = x.shape
    Z = pair.shape[2]
    H = w_bias.shape[1]
    D = C // H
    O = w_sides.shape[1] // 2
    SP = S * N
    R = B * N

    VM = pltpu.VMEM
    x_new = comm_call(
        attention_body, "attention", 1, like((S, B, C)), [x, pair, w_in, w_out, w_bias], 14,
        [VM((N, S, B, C), BF), VM((H, B * B), BF), VM((N, H, B * B), BF), VM((H, B, R), F32),
         VM((S, B, C), F32), VM((S, B, C), F32)],
    )
    edges, mid, gate = comm_call(
        outer_body, "outer", 2,
        [like((N, N, B * B)), like((B, B, Z)), like((B * B, Z), F32)],
        [x_new, pair, w_sides, w_outer, w_tri], 6,
        [VM((B, S, 128), F32), VM((S, B * O), BF), VM((S, B * O), BF), VM((N, S, B * O), BF),
         VM((N, S, B * O), BF), VM((B * O, SP), F32), VM((10 * B, 4 * O * O), BF),
         VM((4 * O * O, 4 * Z), BF), VM((B * B, Z), F32), VM((8, N, B * B), BF), VM((8, N, B * B), BF)],
    )
    pair_new = comm_call(
        triangle_body, "triangle", 3, like((B, B, Z)), [edges, mid, gate, w_tri_out], 9,
        [VM((8, B, R), F32), VM((N, B, R), BF), VM((2, 8, B, R), BF), VM((8, B, R), BF),
         VM((N, B, 8 * B), BF), VM((N, B, 8 * B), BF), VM((N, B, 8 * B), F32), VM((8, N, B * B), BF),
         VM((8, N, B * B), BF)],
    )
    return x_new, pair_new


def solution(mesh):
    tile = P("row", "col", None)
    return jax.shard_map(
        shards,
        mesh=mesh,
        in_specs=(tile, tile) + (P(),) * 7,
        out_specs=(tile, tile),
        check_vma=False,
    )
```

time: 251 us -> 158 us (0.63); the launches traced: 247 us -> 158 us
  local copies, waits for them, and re-layouts: 54.9 us -> 6.1 us
  matrix products: 31.1 us -> 0 us
  other arithmetic: 14.3 us -> 0 us
  Pallas kernels: 145 us -> 151 us
    dot_general x14 -> x0, matrix products: 31.1 us -> none  [the longest x1 13.5 us: shards(): jnp.einsum('shij,sjhd->sihd', e.astype(BF), v, preferred_element_type=F32)]
    reshape x14 -> x0, local copies, waits for them, and re-layouts: 25 us -> none  [the longest x3 12.9 us: shards(): parts = got.reshape(N, N, B, B).transpose(1, 2, 0, 3).reshape(N, B, R)]
    convert_element_type x6 -> x0, local copies, waits for them, and re-layouts: 11.4 us -> none  [the longest x3 10.8 us: shards(): biases.astype(F32)]
    slice x6 -> x0, local copies, waits for them, and re-layouts: 8.77 us -> none  [the longest x2 4.78 us: shards(): v = kv[:, C:].reshape(S, R, H, D)]
    reduce_sum x12 -> x0, other arithmetic: 8.64 us -> none  [the longest x6 4.48 us: standardize(): spread = jnp.mean(center * center, axis=axis, keepdims=True)]
    pallas_call x6 -> x3, Pallas kernels: 145 us -> 151 us  [comm_call(): pl.pallas_call(body, name=name, out_shape=outs, in_specs=[pl.BlockSpec(me...]
    convert_element_type x9 -> x0, other arithmetic: 3.79 us -> none  [the longest x1 1.49 us: shards(): pair_n = standardize(pair).astype(BF).reshape(B * B, Z)]
    unnamed x32 -> x20, local copies, waits for them, and re-layouts: 9.53 us -> 6.1 us
where the time goes in v2:
time: 158 us
  Pallas kernels  151 us (96%)
  local copies, waits for them, and re-layouts  6.1 us (4%)
    pallas_call x3, Pallas kernels, comm_call(): pl.pallas_call(body, name=name, out_shape=outs, in_specs=[pl.BlockSpec(me...  151 us
    unnamed x20, local copies, waits for them, and re-layouts  6.1 us

profile of v2, /device:TPU:8, one launch (start us, length us, event | category | flops | bytes accessed | tf_op | source)
XLA Modules:
  0.0 157.8 jit_solution(15076323161601616581)
XLA Ops:
  0.6 0.0 copy-start.6
  0.6 0.8 copy.11.w_bias
  1.5 0.9 copy.12.w_sides
  2.3 0.0 copy-done.6
  2.4 0.0 copy-start
  2.4 1.0 copy-done
  3.4 0.0 copy-start.2
  3.4 1.0 copy-done.2
  4.4 0.0 copy-start.4
  4.4 0.9 copy-done.4
  5.3 0.0 copy-start.1
  5.3 0.0 copy-start.3
  5.3 0.0 copy-start.5
  5.3 51.0 %attention.1.x_new = bf16[8,40,256]{2,1,0:T(8,128)(2,1)S(1)} custom-call(bf16[8,40,256]{2,1,0:T(8,128)(2,1)S(1)} %copy-done.4, bf16[40,40,128]{2,1,0:T(8,128)(2,1)S(1)} %copy-done, bf16[256,1024]{1,0:T(8,128)(2,1)S(1)} %copy-done.2, bf16[256,256]{1,0:T(8,128)(2,1)S(1)} %copy-done.6, bf16[128,8]{1,0:T(8,128)(2,1)S(1)} %copy.11.w_bias), custom_call_target="tpu_custom_call" | custom-call | tf_op jit(solution)/shard_map/attention/pallas_call | solution.py:86
  56.4 0.0 copy-done.1
  56.4 0.0 copy-done.3
  56.4 0.0 copy-done.5
  56.4 0.0 copy-start.7
  56.4 51.7 %outer.1 = (bf16[16,16,1600]{2,1,0:T(8,128)(2,1)S(1)}, bf16[40,40,128]{2,1,0:T(8,128)(2,1)S(1)}, f32[1600,128]{1,0:T(8,128)S(1)}) custom-call(bf16[8,40,256]{2,1,0:T(8,128)(2,1)S(1)} %attention.1.x_new, bf16[40,40,128]{2,1,0:T(8,128)(2,1)S(1)} %copy-done.1, bf16[256,64]{1,0:T(8,128)(2,1)S(1)} %copy.12.w_sides, bf16[1024,128]{1,0:T(8,128)(2,1)S(1)} %copy-done.3, ...), custom_call_target="tpu_custom_call" | custom-call | tf_op jit(solution)/shard_map/outer/pallas_call | solution.py:86
  108.1 0.0 copy-done.7
  108.1 48.3 %triangle.1 = bf16[40,40,128]{2,1,0:T(8,128)(2,1)S(1)} custom-call(bf16[16,16,1600]{2,1,0:T(8,128)(2,1)S(1)} %get-tuple-element.5.edges, bf16[40,40,128]{2,1,0:T(8,128)(2,1)S(1)} %get-tuple-element.6.mid, f32[1600,128]{1,0:T(8,128)S(1)} %get-tuple-element.7.gate, bf16[128,128]{1,0:T(8,128)(2,1)S(1)} %copy-done.7), custom_call_target="tpu_custom_call" | custom-call | tf_op jit(solution)/shard_map/triangle/pallas_call | solution.py:86
  156.4 0.7 copy.15
  157.1 0.8 copy.16
Async XLA Ops:
  0.6 1.7 %copy-start.6 = (bf16[256,256]{1,0:T(8,128)(2,1)S(1)}, bf16[256,256]{1,0:T(8,128)(2,1)}, u32[]{:S(2)}) copy-start(bf16[256,256]{1,0:T(8,128)(2,1)} %w_out.1) | copy-start | bytes 393220
  2.4 1.0 copy-start
  3.4 1.0 copy-start.2
  4.4 0.9 copy-start.4
  5.3 51.0 %copy-start.1 = (bf16[40,40,128]{2,1,0:T(8,128)(2,1)S(1)}, bf16[40,40,128]{2,1,0:T(8,128)(2,1)}, u32[]{:S(2)}) copy-start(bf16[40,40,128]{2,1,0:T(8,128)(2,1)} %pair.3) | copy-start | bytes 1228804
  5.3 51.0 %copy-start.3 = (bf16[1024,128]{1,0:T(8,128)(2,1)S(1)}, bf16[1024,128]{1,0:T(8,128)(2,1)}, u32[]{:S(2)}) copy-start(bf16[1024,128]{1,0:T(8,128)(2,1)} %w_outer.1) | copy-start | bytes 786436
  5.3 51.1 %copy-start.5 = (bf16[128,640]{1,0:T(8,128)(2,1)S(1)}, bf16[128,640]{1,0:T(8,128)(2,1)}, u32[]{:S(2)}) copy-start(bf16[128,640]{1,0:T(8,128)(2,1)} %w_tri.1) | copy-start | bytes 491524
  56.4 51.7 %copy-start.7 = (bf16[128,128]{1,0:T(8,128)(2,1)S(1)}, bf16[128,128]{1,0:T(8,128)(2,1)}, u32[]{:S(2)}) copy-start(bf16[128,128]{1,0:T(8,128)(2,1)} %w.1) | copy-start | bytes 98308

commit v3 on v2

--- a/solution.py
+++ b/solution.py
@@ -45,32 +45,29 @@
     pl.semaphore_wait(pltpu.get_barrier_semaphore(), count)
 
 
-def turned_greet(by_row):
+def turned_greet():
     r, c = here()
     for s in range(N):
         k = lax.rem(c + s, N)
-        to = (c, k) if by_row else (k, r)
 
         @pl.when((c != r) | (k != c))
         def _():
-            greet(to)
-
-
-def turned_push(src, dst, send, recv, by_row):
-    r, c = here()
-    slot = dst.at[c] if by_row else dst.at[r]
+            greet((c, k))
+
+
+def turned_push(src, dst, send, recv):
+    r, c = here()
     for s in range(N):
-        k = lax.rem(r + s, N)
+        k = lax.rem(r + c + s, N)
         own = (k == r) & (r == c)
-        to = (k, r) if by_row else (c, k)
 
         @pl.when(jnp.logical_not(own))
         def _():
-            push(src, slot, send, recv, to)
+            push(src, dst.at[c], send, recv, (k, r))
 
         @pl.when(own)
         def _():
-            local(src, slot, recv)
+            local(src, dst.at[c], recv)
 
 
 def turned_sent(dst, send):
@@ -97,50 +94,56 @@
 
 
 def attention_body(
-    x, pair, w_in, w_out, w_bias, x_new, xs, bias_out, biases, bias, q_all, gates, sem
+    x, pair, w_in, w_out, w_bias, x_new, xs, bias_out, biases, bias, q_all, gates, near, far, sem
 ):
     r, c = here()
     core = lax.rem(c, 2)
     mate = c + 1 - 2 * core
     S, B, C = x.shape
-    H = w_bias.shape[1]
+    H = w_bias.shape[0]
     D = C // H
+    mine = c // 2
     for s in range(1, 8):
         greet((r, lax.rem(c + 2 * s, N)))
     greet((r, mate))
-    turned_greet(True)
-    greeted(8 + 15 + jnp.where(r == c, 0, 1))
-    for s in range(1, 8):
-        push(x, xs.at[c], sem.at[0], sem.at[2 + s], (r, lax.rem(c + 2 * s, N)))
-    push(x, xs.at[c], sem.at[10], sem.at[2], (r, mate))
-    local(x, xs.at[c], sem.at[11])
+    turned_greet()
     pair_n = standardize(pair[...]).astype(BF).reshape(B * B, pair.shape[2])
     bias_out[...] = lax.dot_general(
-        w_bias[...], pair_n, (((0,), (1,)), ((), ())), preferred_element_type=F32
+        w_bias[...], pair_n, (((1,), (1,)), ((), ())), preferred_element_type=F32
     ).astype(BF)
-    turned_push(bias_out, biases, sem.at[12], sem.at[13], True)
+    greeted(8 + 15 + jnp.where(r == c, 0, 1))
+    turned_push(bias_out, biases, sem.at[0], sem.at[1])
+
+    @pl.loop(0, S)
+    def _(s):
+        for g in range(1, 8):
+            push(x.at[s], xs.at[s, core, mine], sem.at[2], near.at[s], (r, lax.rem(c + 2 * g, N)))
+        local(x.at[s], xs.at[s, core, mine], near.at[s])
+
+    def forward(s):
+        drain(xs.at[s, core], near.at[s])
+        push(xs.at[s, core], xs.at[s, core], sem.at[3], far.at[s], (r, mate))
+
     own_n = standardize(x[...]).astype(BF).reshape(S * B, C)
     q = jnp.dot(own_n, w_in[:, :C], preferred_element_type=F32) * D ** (-0.5)
     q_all[...] = q.reshape(S, B, C)
     gates[...] = jax.nn.sigmoid(
         jnp.dot(own_n, w_in[:, 3 * C :], preferred_element_type=F32)
     ).reshape(S, B, C)
-    for s in range(1, 8):
-        source = lax.rem(c - 2 * s + 2 * N, N)
-        drain(xs.at[source], sem.at[2 + s])
-        push(xs.at[source], xs.at[source], sem.at[10], sem.at[2], (r, mate))
-    turned_sent(biases, sem.at[12])
-    drain(biases, sem.at[13])
-    spread(lambda k: biases[k].astype(F32), bias, B)
-    drain(xs.at[pl.ds(0, 7)], sem.at[0])
-    drain(xs.at[pl.ds(0, 8)], sem.at[10])
-    drain(xs.at[pl.ds(0, 8)], sem.at[2])
-    drain(xs.at[0], sem.at[11])
+    forward(0)
+    turned_sent(biases, sem.at[0])
+    drain(biases, sem.at[1])
+    spread(lambda k: biases[2 * (k % 8) + k // 8].astype(F32), bias, B)
     head = lax.broadcasted_iota(jnp.int32, (B, C), 1) // D
 
     @pl.loop(0, S)
     def _(s):
-        x_s = standardize(xs[:, s]).reshape(N * B, C).astype(BF)
+        @pl.when(s < S - 1)
+        def _():
+            forward(s + 1)
+
+        drain(xs.at[s, 1 - core], far.at[s])
+        x_s = standardize(xs[s]).reshape(N * B, C).astype(BF)
         k = jnp.dot(x_s, w_in[:, C : 2 * C], preferred_element_type=F32).astype(BF)
         v = jnp.dot(x_s, w_in[:, 2 * C : 3 * C], preferred_element_type=F32).astype(BF)
         q_s = q_all[s]
@@ -159,6 +162,10 @@
             x[s].astype(F32) + jnp.dot(gated, w_out[...], preferred_element_type=F32)
         ).astype(BF)
 
+    for g in range(7):
+        drain(x, sem.at[2])
+    drain(xs.at[:, 0], sem.at[3])
+
 
 def spread(block, out, B):
     blocks = [block(k) for k in range(N)]
@@ -168,29 +175,60 @@
 
 def outer_body(
     x_new, pair, w_sides, w_outer, w_tri, got, mid, gate,
-    by_residue, left, right, lefts, rights, tall, stacked, w_wide, normed, left_edge, right_edge, sem,
+    flat, left, right, chunk, lefts, rights, left_s, right_s, tall, stacked, w_wide, normed,
+    left_edge, right_edge, sem,
 ):
     r, c = here()
+    core = lax.rem(c, 2)
+    mate = c + 1 - 2 * core
+    mine = c // 2
+    parity = lax.rem(r, 2)
     S, B, C = x_new.shape
-    O = w_sides.shape[1] // 2
+    O = w_sides.shape[0] // 2
     Z = pair.shape[2]
+    G = B // 4
     for s in range(1, N):
         greet((lax.rem(r + s, N), c))
-    turned_greet(False)
     for s in range(1, N):
         greet((r, lax.rem(c + s, N)))
-    sides = jnp.dot(
-        standardize(x_new[...]).astype(BF).reshape(S * B, C), w_sides[...], preferred_element_type=F32
-    )
-    for s in range(S):
-        by_residue[:, s, : 2 * O] = sides[s * B : (s + 1) * B]
-    left[...] = jnp.concatenate([by_residue[i, :, :O] for i in range(B)], 1).astype(BF)
-    right[...] = jnp.concatenate([by_residue[i, :, O : 2 * O] for i in range(B)], 1).astype(BF)
-    greeted(45 + jnp.where(r == c, 0, 1))
-    turned_push(left, lefts, sem.at[0], sem.at[1], False)
+    for s in range(8):
+        k = 2 * lax.rem(mine + s, 8) + core
+
+        @pl.when((k != r) | (r != c))
+        def _():
+            greet((k, r))
+
+    flat[:, : 2 * O] = lax.dot_general(
+        standardize(x_new[...]).astype(BF).reshape(S * B, C), w_sides[...],
+        (((1,), (1,)), ((), ())), preferred_element_type=F32,
+    )
+    for k, side in ((0, left), (O, right)):
+        lanes = jnp.concatenate(
+            [flat[pl.ds(u, S * G, stride=4), :][:, k : k + O] for u in range(4)], 1
+        )
+        for s in range(S):
+            side[s] = lanes[s * G : (s + 1) * G].astype(BF)
+    greeted(38 - jnp.where(r == c, 1, 0))
+    for s in range(8):
+        g = lax.rem(r // 2 + s, 8)
+        k = 2 * g + parity
+        own = (k == c) & (r == c)
+
+        @pl.when(jnp.logical_not(own))
+        def _():
+            push(left.at[g], chunk.at[r // 2], sem.at[0], sem.at[1], (c, k))
+
+        @pl.when(own)
+        def _():
+            local(left.at[g], chunk.at[r // 2], sem.at[1])
+
     for s in range(1, N):
-        push(right, rights.at[r], sem.at[2], sem.at[3], (lax.rem(r + s, N), c))
-    local(right, rights.at[r], sem.at[3])
+        push(right, rights.at[parity, :, r // 2], sem.at[2], sem.at[3], (lax.rem(r + s, N), c))
+    local(right, rights.at[parity, :, r // 2], sem.at[3])
+    drain(chunk, sem.at[1])
+    for s in range(1, 8):
+        push(chunk, lefts.at[core, mine], sem.at[6], sem.at[7], (r, lax.rem(c + 2 * s, N)))
+    local(chunk, lefts.at[core, mine], sem.at[7])
 
     w_wide[...] = jnp.zeros_like(w_wide)
     tall[pl.ds(0, O * O), :] = w_outer[...].astype(F32)
@@ -198,19 +236,29 @@
         part = tall[pl.ds(d, O, stride=O), :].astype(BF)
         for i in range(4):
             w_wide[pl.ds(d * 4 * O + i * O, O), i * Z : (i + 1) * Z] = part
-    turned_sent(lefts, sem.at[0])
-    drain(lefts, sem.at[1])
-    drain(rights.at[pl.ds(0, N - 1)], sem.at[2])
+    drain(lefts.at[core], sem.at[7])
+    push(lefts.at[core], lefts.at[core], sem.at[8], sem.at[9], (r, mate))
+    drain(chunk.at[pl.ds(0, 7)], sem.at[0])
+
+    @pl.when(r != c)
+    def _():
+        drain(chunk.at[0], sem.at[0])
+
+    for s in range(N - 1):
+        drain(right, sem.at[2])
+    drain(lefts.at[0, pl.ds(0, 7)], sem.at[6])
     drain(rights, sem.at[3])
-
-    tall[...] = rights[...].reshape(S * N, B * O).astype(F32).T
+    right_s[...] = rights[...].astype(F32).reshape(S * N, G, 4 * O)
+    for k in range(G):
+        tall[pl.ds(k * 4 * O, 4 * O), :] = right_s[:, k, :].T
     right_t = jnp.concatenate([tall[pl.ds(d, B, stride=O), :] for d in range(O)], 0).astype(BF)
-    left_s = lefts[...].reshape(S * N, B * O)
+    drain(lefts.at[0], sem.at[8])
+    drain(lefts.at[1 - core], sem.at[9])
+    left_s[...] = lefts[...].astype(F32).reshape(S * N, G, 4 * O)
     for g in range(B // 8):
         halves = [
-            jnp.dot(
-                right_t, left_s[:, k * 4 * O : (k + 1) * 4 * O], preferred_element_type=F32
-            ) * (1.0 / (S * N))
+            jnp.dot(right_t, left_s[:, k, :].astype(BF), preferred_element_type=F32)
+            * (1.0 / (S * N))
             for k in (2 * g, 2 * g + 1)
         ]
         for d in range(O):
@@ -230,7 +278,6 @@
         both = lax.dot_general(w, tri_n, (((0,), (1,)), ((), ())), preferred_element_type=F32)
         return (jax.nn.sigmoid(both[Z:]) * both[:Z]).astype(BF).reshape(8, N, B * B)
 
-    parity = lax.rem(r, 2)
     for k, ref in ((0, left_edge), (1, right_edge)):
         ref[...] = edge(k)
         for s in range(8):
@@ -338,23 +385,25 @@
     S, B, C = x.shape
     Z = pair.shape[2]
     H = w_bias.shape[1]
-    D = C // H
     O = w_sides.shape[1] // 2
+    G = B // 4
     SP = S * N
     R = B * N
 
     VM = pltpu.VMEM
     x_new = comm_call(
-        attention_body, "attention", 1, like((S, B, C)), [x, pair, w_in, w_out, w_bias], 14,
-        [VM((N, S, B, C), BF), VM((H, B * B), BF), VM((N, H, B * B), BF), VM((H, B, R), F32),
-         VM((S, B, C), F32), VM((S, B, C), F32)],
+        attention_body, "attention", 1, like((S, B, C)), [x, pair, w_in, w_out, w_bias.T], 4,
+        [VM((S, 2, 8, B, C), BF), VM((H, B * B), BF), VM((N, H, B * B), BF), VM((H, B, R), F32),
+         VM((S, B, C), F32), VM((S, B, C), F32),
+         pltpu.SemaphoreType.DMA((S,)), pltpu.SemaphoreType.DMA((S,))],
     )
     edges, mid, gate = comm_call(
         outer_body, "outer", 2,
         [like((N, N, B * B)), like((B, B, Z)), like((B * B, Z), F32)],
-        [x_new, pair, w_sides, w_outer, w_tri], 6,
-        [VM((B, S, 128), F32), VM((S, B * O), BF), VM((S, B * O), BF), VM((N, S, B * O), BF),
-         VM((N, S, B * O), BF), VM((B * O, SP), F32), VM((10 * B, 4 * O * O), BF),
+        [x_new, pair, w_sides.T, w_outer, w_tri], 10,
+        [VM((S * B, 128), F32), VM((S, G, 4 * O), BF), VM((S, G, 4 * O), BF), VM((8, G, 4 * O), BF),
+         VM((2, S, 8, G, 4 * O), BF), VM((2, S, 8, G, 4 * O), BF), VM((SP, G, 4 * O), F32),
+         VM((SP, G, 4 * O), F32), VM((B * O, SP), F32), VM((10 * B, 4 * O * O), BF),
          VM((4 * O * O, 4 * Z), BF), VM((B * B, Z), F32), VM((8, N, B * B), BF), VM((8, N, B * B), BF)],
     )
     pair_new = comm_call(

time: 158 us -> 133 us (0.84)
  Pallas kernels: 151 us -> 126 us
    pallas_call x3, Pallas kernels: 151 us -> 126 us  [comm_call(): pl.pallas_call(body, name=name, out_shape=outs, in_specs=[pl.BlockSpec(me...]
    unnamed x20 -> x22, local copies, waits for them, and re-layouts: 6.1 us -> 5.98 us
where the time goes in v3:
time: 133 us
  Pallas kernels  126 us (95%)
  local copies, waits for them, and re-layouts  5.98 us (4%)
    pallas_call x3, Pallas kernels, comm_call(): pl.pallas_call(body, name=name, out_shape=outs, in_specs=[pl.BlockSpec(me...  126 us
    unnamed x22, local copies, waits for them, and re-layouts  5.98 us

profile of v3, /device:TPU:8, one launch (start us, length us, event | category | flops | bytes accessed | tf_op | source)
XLA Modules:
  0.0 133.1 jit_solution(10795553418778859345)
XLA Ops:
  0.6 0.0 copy-start.9
  0.6 0.7 copy-done.9
  1.3 0.0 copy-start
  1.3 1.0 copy-done
  2.3 0.0 copy-start.2
  2.3 1.0 copy-done.2
  3.4 0.0 copy-start.5
  3.4 0.9 copy-done.5
  4.3 0.0 copy-start.6
  4.3 0.9 copy-done.6
  5.2 0.0 copy-start.1
  5.2 0.0 copy-start.3
  5.2 0.0 copy-start.4
  5.2 0.0 copy-start.8
  5.2 42.1 %attention.1.x_new = bf16[8,40,256]{2,1,0:T(8,128)(2,1)S(1)} custom-call(bf16[8,40,256]{2,1,0:T(8,128)(2,1)S(1)} %copy-done.5, bf16[40,40,128]{2,1,0:T(8,128)(2,1)S(1)} %copy-done, bf16[256,1024]{1,0:T(8,128)(2,1)S(1)} %copy-done.2, bf16[256,256]{1,0:T(8,128)(2,1)S(1)} %copy-done.6, bf16[8,128]{1,0:T(8,128)(2,1)S(1)} %bitcast.3), custom_call_target="tpu_custom_call" | custom-call | tf_op jit(solution)/shard_map/attention/pallas_call | solution.py:83
  47.3 0.0 copy-done.1
  47.3 0.0 copy-done.3
  47.3 0.0 copy-done.4
  47.3 0.0 copy-done.8
  47.3 0.0 copy-start.7
  47.3 34.6 %outer.1 = (bf16[16,16,1600]{2,1,0:T(8,128)(2,1)S(1)}, bf16[40,40,128]{2,1,0:T(8,128)(2,1)S(1)}, f32[1600,128]{1,0:T(8,128)S(1)}) custom-call(bf16[8,40,256]{2,1,0:T(8,128)(2,1)S(1)} %attention.1.x_new, bf16[40,40,128]{2,1,0:T(8,128)(2,1)S(1)} %copy-done.1, bf16[64,256]{1,0:T(8,128)(2,1)S(1)} %bitcast.2, bf16[1024,128]{1,0:T(8,128)(2,1)S(1)} %copy-done.3, ...), custom_call_target="tpu_custom_call" | custom-call | tf_op jit(solution)/shard_map/outer/pallas_call | solution.py:83
  81.9 0.0 copy-done.7
  81.9 49.8 %triangle.1 = bf16[40,40,128]{2,1,0:T(8,128)(2,1)S(1)} custom-call(bf16[16,16,1600]{2,1,0:T(8,128)(2,1)S(1)} %get-tuple-element.5.edges, bf16[40,40,128]{2,1,0:T(8,128)(2,1)S(1)} %get-tuple-element.6.mid, f32[1600,128]{1,0:T(8,128)S(1)} %get-tuple-element.7.gate, bf16[128,128]{1,0:T(8,128)(2,1)S(1)} %copy-done.7), custom_call_target="tpu_custom_call" | custom-call | tf_op jit(solution)/shard_map/triangle/pallas_call | solution.py:83
  131.7 0.7 copy.13
  132.4 0.8 copy.14
Async XLA Ops:
  0.6 0.7 copy-start.9
  1.3 1.0 copy-start
  2.3 1.0 copy-start.2
  3.4 0.9 copy-start.5
  4.3 0.9 copy-start.6
  5.2 42.1 %copy-start.1 = (bf16[40,40,128]{2,1,0:T(8,128)(2,1)S(1)}, bf16[40,40,128]{2,1,0:T(8,128)(2,1)}, u32[]{:S(2)}) copy-start(bf16[40,40,128]{2,1,0:T(8,128)(2,1)} %pair.3) | copy-start | bytes 1228804
  5.2 42.1 %copy-start.3 = (bf16[1024,128]{1,0:T(8,128)(2,1)S(1)}, bf16[1024,128]{1,0:T(8,128)(2,1)}, u32[]{:S(2)}) copy-start(bf16[1024,128]{1,0:T(8,128)(2,1)} %w_outer.1) | copy-start | bytes 786436
  5.2 42.1 %copy-start.4 = (bf16[128,640]{1,0:T(8,128)(2,1)S(1)}, bf16[128,640]{1,0:T(8,128)(2,1)}, u32[]{:S(2)}) copy-start(bf16[128,640]{1,0:T(8,128)(2,1)} %w_tri.1) | copy-start | bytes 491524
  5.2 42.1 %copy-start.8 = (bf16[256,64]{0,1:T(8,128)(2,1)S(1)}, bf16[256,64]{0,1:T(8,128)(2,1)}, u32[]{:S(2)}) copy-start(bf16[256,64]{0,1:T(8,128)(2,1)} %param.14) | copy-start | bytes 98308
  47.3 34.6 %copy-start.7 = (bf16[128,128]{1,0:T(8,128)(2,1)S(1)}, bf16[128,128]{1,0:T(8,128)(2,1)}, u32[]{:S(2)}) copy-start(bf16[128,128]{1,0:T(8,128)(2,1)} %w.1) | copy-start | bytes 98308

commit v4 on v3

v4 whole, which is shorter than its diff:
```python
import functools

import jax
import jax.numpy as jnp
from jax import lax
from jax.experimental import pallas as pl
from jax.experimental.pallas import tpu as pltpu
from jax.sharding import PartitionSpec

MESH = pl.DeviceIdType.MESH
EPS = 1e-05
N = 16
BF = jnp.bfloat16
F32 = jnp.float32


def standardize(v, axis=-1):
    v = v.astype(F32)
    center = v - jnp.mean(v, axis=axis, keepdims=True)
    spread = jnp.mean(center * center, axis=axis, keepdims=True)
    return center * lax.rsqrt(spread + EPS)


def here():
    return lax.axis_index("row"), lax.axis_index("col")


def push(src, dst, send, recv, to):
    pltpu.make_async_remote_copy(src, dst, send, recv, device_id=to, device_id_type=MESH).start()


def local(src, dst, recv):
    pltpu.make_async_copy(src, dst, recv).start()


def drain(ref, sem):
    pltpu.make_async_copy(ref, ref, sem).wait()


def greet(to):
    pl.semaphore_signal(pltpu.get_barrier_semaphore(), inc=1, device_id=to, device_id_type=MESH)


def greeted(count):
    pl.semaphore_wait(pltpu.get_barrier_semaphore(), count)


def comm_call(body, name, collective_id, outs, ins, sems, scratch=(), place=pltpu.VMEM):
    return pl.pallas_call(
        body,
        name=name,
        out_shape=outs,
        in_specs=[pl.BlockSpec(memory_space=place)] * len(ins),
        out_specs=[pl.BlockSpec(memory_space=place)] * len(outs),
        scratch_shapes=[*scratch, pltpu.SemaphoreType.DMA((sems,))],
        compiler_params=pltpu.CompilerParams(
            collective_id=collective_id, has_side_effects=True, vmem_limit_bytes=62 << 20
        ),
    )(*ins)


def block_body(
    x_in, pair_in, w_in_in, w_out_in, w_bias_in, w_sides_in, w_outer_in, w_tri_in, w_last_in,
    x_out, pair_out,
    x, pair, w_in, w_out, w_bias, w_sides, w_outer, w_tri, w_last,
    x_new, got, mid, gate, pair_new, xs, bias_out, bias_in, biases, bias, q_all, gates, v_all, scores_all, gated,
    flat, left, right, chunk, lefts, rights, left_s, right_s, tall, stacked, w_wide, normed,
    left_edge, right_edge, spreads, parts, held, mates, sums, channel, back, outgoing, tiles,
    near, far, load, back_sem, sem,
):
    r, c = here()
    core = lax.rem(c, 2)
    mate = c + 1 - 2 * core
    mine = c // 2
    parity = lax.rem(r, 2)
    S, B, C = x.shape
    H = w_bias.shape[0]
    D = C // H
    O = w_sides.shape[0] // 2
    Z = pair.shape[2]
    G = B // 4
    P = bias_out.shape[0]
    loads = [
        pltpu.make_async_copy(src, dst, load.at[k])
        for k, (src, dst) in enumerate(
            (
                (pair_in, pair), (w_bias_in, w_bias), (x_in, x), (w_in_in, w_in), (w_out_in, w_out),
                (w_sides_in, w_sides), (w_outer_in, w_outer), (w_tri_in, w_tri),
                (w_last_in, w_last),
            )
        )
    ]
    for cp in loads:
        cp.start()
    for s in range(1, N):
        greet((r, lax.rem(c + s, N)))
    for s in range(1, N):
        greet((lax.rem(r + s, N), c))

    @pl.when(r < P)
    def _():
        for s in range(N):
            k = lax.rem(c + s, N)

            @pl.when((c != r) | (k != c))
            def _():
                greet((c, k))

    for s in range(8):
        k = 2 * lax.rem(mine + s, 8) + core

        @pl.when((k != r) | (r != c))
        def _():
            greet((k, r))

    loads[0].wait()
    loads[1].wait()
    pair_n = standardize(pair[...]).astype(BF).reshape(B * B, Z)
    bias_flat = lax.dot_general(
        w_bias[...], pair_n, (((1,), (1,)), ((), ())), preferred_element_type=F32
    )
    bias_flat = jnp.concatenate([bias_flat, jnp.zeros((H, P * 128 - B * B), F32)], 1).astype(BF)
    for k in range(P):
        bias_out[k] = bias_flat[:, k * 128 : (k + 1) * 128]
    own_p = (r == c) & (r < P)
    greeted(38 + P - jnp.where(r == c, 1, 0) - jnp.where(own_p, 1, 0))
    for s in range(P):
        k = lax.rem(s + c, P)
        own = (k == r) & (r == c)

        @pl.when(jnp.logical_not(own))
        def _():
            push(bias_out.at[k], bias_in.at[c], sem.at[10], sem.at[11], (k, r))

        @pl.when(own)
        def _():
            local(bias_out.at[k], bias_in.at[c], sem.at[11])

    @pl.loop(0, S)
    def _(s):
        for g in range(1, 8):
            push(x_in.at[s], xs.at[s, core, mine], sem.at[12], near.at[s], (r, lax.rem(c + 2 * g, N)))
        local(x_in.at[s], xs.at[s, core, mine], near.at[s])

    @pl.when(r < P)
    def _():
        drain(bias_in, sem.at[11])
        for s in range(1, N):
            push(bias_in, biases.at[r], sem.at[4], sem.at[5], (lax.rem(r + s, N), c))
        local(bias_in, biases.at[r], sem.at[5])

    def forward(s):
        drain(xs.at[s, core], near.at[s])
        push(xs.at[s, core], xs.at[s, core], sem.at[13], far.at[s], (r, mate))

    for cp in loads[2:]:
        cp.wait()
    own_n = standardize(x[...]).astype(BF).reshape(S * B, C)
    q = jnp.dot(own_n, w_in[:, :C], preferred_element_type=F32) * D ** (-0.5)
    q_all[...] = q.reshape(S, B, C)
    gates[...] = jax.nn.sigmoid(jnp.dot(own_n, w_in[:, 3 * C :], preferred_element_type=F32))
    w_wide[...] = jnp.zeros_like(w_wide)
    tall[pl.ds(0, O * O), :] = w_outer[...].astype(F32)
    for d in range(O):
        part = tall[pl.ds(d, O, stride=O), :].astype(BF)
        for i in range(4):
            w_wide[pl.ds(d * 4 * O + i * O, O), i * Z : (i + 1) * Z] = part
    head = lax.broadcasted_iota(jnp.int32, (B, C), 1) // D
    forward(0)

    @pl.loop(0, S)
    def _(s):
        @pl.when(s < S - 1)
        def _():
            forward(s + 1)

        drain(xs.at[s, 1 - core], far.at[s])
        x_s = standardize(xs[s]).reshape(N * B, C).astype(BF)
        k = jnp.dot(x_s, w_in[:, C : 2 * C], preferred_element_type=F32).astype(BF)
        v_all[s] = jnp.dot(x_s, w_in[:, 2 * C : 3 * C], preferred_element_type=F32).astype(BF)
        q_s = q_all[s]
        q_h = jnp.concatenate([jnp.where(head == h, q_s, 0.0) for h in range(H)], 0).astype(BF)
        scores_all[s] = lax.dot_general(
            q_h, k, (((1,), (1,)), ((), ())), preferred_element_type=F32
        )

    drain(bias_out.at[pl.ds(0, P - 1)], sem.at[10])

    @pl.when(jnp.logical_not(own_p))
    def _():
        drain(bias_out.at[0], sem.at[10])

    @pl.when(r < P)
    def _():
        for s in range(1, N):
            drain(bias_in, sem.at[4])

    drain(biases, sem.at[5])

    def bias_of(k):
        block = 2 * (k % 8) + k // 8
        return jnp.concatenate([biases[p, block].astype(F32) for p in range(P)], 1)

    spread(bias_of, bias, B)
    for half in range(2):
        first, count = half * S // 2, S // 2

        @pl.loop(first, first + count)
        def _(s):
            scores = scores_all[s] + bias[...].reshape(H * B, N * B)
            e = jnp.exp(scores - jnp.max(scores, -1, keepdims=True))
            att = jnp.dot(e.astype(BF), v_all[s], preferred_element_type=F32)
            att = (att / jnp.sum(e, -1, keepdims=True)).reshape(H, B, C)
            total = jnp.where(head == 0, att[0], 0.0)
            for h in range(1, H):
                total = jnp.where(head == h, att[h], total)
            gated[pl.ds(pl.multiple_of(s * B, 8), B), :] = total

        span = slice(first * B, (first + count) * B)
        update = jnp.dot(
            (gated[span] * gates[span]).astype(BF), w_out[...], preferred_element_type=F32
        )
        x_half = (
            x[first : first + count].astype(F32) + update.reshape(count, B, C)
        ).astype(BF)
        x_new[first : first + count] = x_half
        flat[span, : 2 * O] = lax.dot_general(
            standardize(x_half).astype(BF).reshape(count * B, C), w_sides[...],
            (((1,), (1,)), ((), ())), preferred_element_type=F32,
        )
        for k, side in ((0, left), (O, right)):
            lanes = jnp.concatenate(
                [flat[pl.ds(first * B + u, count * G, stride=4), :][:, k : k + O] for u in range(4)], 1
            )
            for s in range(count):
                side[first + s] = lanes[s * G : (s + 1) * G].astype(BF)
        for s in range(first, first + count):
            k = 2 * s + parity
            own = (k == c) & (r == c)

            @pl.when(jnp.logical_not(own))
            def _():
                push(left.at[s], chunk.at[r // 2], sem.at[0], sem.at[1], (c, k))

            @pl.when(own)
            def _():
                local(left.at[s], chunk.at[r // 2], sem.at[1])

        part = right.at[pl.ds(first, count)]
        there = rights.at[parity, pl.ds(first, count), r // 2]
        for s in range(1, N):
            push(part, there, sem.at[2], sem.at[3], (lax.rem(r + s, N), c))
        local(part, there, sem.at[3])
    x_done = pltpu.make_async_copy(x_new, x_out, load.at[0])
    x_done.start()
    drain(chunk, sem.at[1])
    for s in range(1, 8):
        push(chunk, lefts.at[core, mine], sem.at[6], sem.at[7], (r, lax.rem(c + 2 * s, N)))
    local(chunk, lefts.at[core, mine], sem.at[7])
    for g in range(7):
        drain(xs.at[:, 0, 0], sem.at[12])
    drain(xs.at[:, 0], sem.at[13])
    drain(lefts.at[core], sem.at[7])
    push(lefts.at[core], lefts.at[core], sem.at[8], sem.at[9], (r, mate))
    drain(chunk.at[pl.ds(0, 7)], sem.at[0])

    @pl.when(r != c)
    def _():
        drain(chunk.at[0], sem.at[0])

    for s in range(N - 1):
        drain(right, sem.at[2])
    drain(lefts.at[0, pl.ds(0, 7)], sem.at[6])
    drain(rights, sem.at[3])
    right_s[...] = rights[...].astype(F32).reshape(S * N, G, 4 * O)
    for k in range(G):
        tall[pl.ds(k * 4 * O, 4 * O), :] = right_s[:, k, :].T
    right_t = jnp.concatenate([tall[pl.ds(d, B, stride=O), :] for d in range(O)], 0).astype(BF)
    drain(lefts.at[0], sem.at[8])
    drain(lefts.at[1 - core], sem.at[9])
    left_s[...] = lefts[...].astype(F32).reshape(S * N, G, 4 * O)
    for g in range(B // 8):
        halves = [
            jnp.dot(right_t, left_s[:, k, :].astype(BF), preferred_element_type=F32)
            * (1.0 / (S * N))
            for k in (2 * g, 2 * g + 1)
        ]
        for d in range(O):
            stacked[pl.ds(g * 2 * B, 2 * B), d * 4 * O : (d + 1) * 4 * O] = jnp.concatenate(
                [h[d * B : (d + 1) * B] for h in halves], 0
            ).astype(BF)
    wide = jnp.dot(stacked[...], w_wide[...], preferred_element_type=F32)
    for i in range(B):
        k, u = i // 4, i % 4
        row = (pair[i].astype(F32) + wide[k * B : (k + 1) * B, u * Z : (u + 1) * Z]).astype(BF)
        mid[i] = row
        normed[pl.ds(i * B, B), :] = standardize(row)
    tri_n = normed[...].astype(BF)

    def edge(k):
        w = w_tri[:, 2 * k * Z : 2 * (k + 1) * Z]
        both = lax.dot_general(w, tri_n, (((0,), (1,)), ((), ())), preferred_element_type=F32)
        return (jax.nn.sigmoid(both[Z:]) * both[:Z]).astype(BF).reshape(8, N, B * B)

    for k, ref in ((0, left_edge), (1, right_edge)):
        ref[...] = edge(k)
        for s in range(8):
            g = lax.rem(c // 2 + s, 8)
            to = 2 * g + lax.rem(parity + 1 + k, 2)
            if s == 0:

                @pl.when(to != c)
                def _():
                    push(ref.at[g], got.at[c], sem.at[14], sem.at[15], (r, to))

                @pl.when(to == c)
                def _():
                    local(ref.at[g], got.at[c], sem.at[15])
            else:
                push(ref.at[g], got.at[c], sem.at[14], sem.at[15], (r, to))
    gate[...] = jax.nn.sigmoid(jnp.dot(tri_n, w_tri[:, 4 * Z :], preferred_element_type=F32))
    drain(got.at[pl.ds(0, N - 1)], sem.at[14])
    drain(got, sem.at[15])
    kind = lax.rem(r + core, 2)
    R = N * B
    for h in range(2):
        spread(lambda k: got[k].astype(F32)[8 * h : 8 * h + 8], spreads, B)
        parts[pl.ds(8 * h, 8)] = spreads[...].astype(BF)
        arrived = back_sem.at[1 + lax.rem(r, 2)]
        for s in range(8):
            q = 8 * h + lax.rem(r + s, 8)
            if s == 0:

                @pl.when(q != r)
                def _():
                    push(parts.at[q], held.at[kind, r // 2], back_sem.at[0], arrived, (q, c))

                @pl.when(q == r)
                def _():
                    local(parts.at[q], held.at[kind, r // 2], arrived)
            else:
                push(parts.at[q], held.at[kind, r // 2], back_sem.at[0], arrived, (q, c))
    drain(held.at[1], back_sem.at[2 - core])
    push(held.at[1], mates, back_sem.at[3], back_sem.at[4], (r, mate))
    drain(held.at[0], back_sem.at[1 + core])
    columns = held[0].reshape(8 * B, R)
    for rows, parity in ((held.at[1], 1 - core), (mates, core)):
        if rows is mates:
            drain(mates, back_sem.at[4])
        total = lax.dot_general(
            rows[...].reshape(8 * B, R), columns, (((1,), (1,)), ((), ())), preferred_element_type=F32
        )
        for s in range(8):
            q = 2 * s + parity
            sums[q] = total[s * B : (s + 1) * B].astype(BF)

            @pl.when(q != r)
            def _():
                push(sums.at[q], channel.at[r], back_sem.at[5], back_sem.at[6], (q, c))

            @pl.when(q == r)
            def _():
                local(sums.at[q], channel.at[r], back_sem.at[6])
    drain(parts.at[pl.ds(0, N - 1)], back_sem.at[0])
    drain(mates, back_sem.at[3])
    drain(sums.at[pl.ds(0, N - 1)], back_sem.at[5])
    drain(channel, back_sem.at[6])
    back[...] = channel[...].astype(F32)
    rows = [back[:, i, :] for i in range(B)]
    for g in range(8):
        outgoing[g] = jnp.concatenate([v[:, g * B : (g + 1) * B] for v in rows], 1).astype(BF)
    for s in range(1, 8):
        g = lax.rem(mine + s, 8)
        push(outgoing.at[g], tiles.at[mine], back_sem.at[7], back_sem.at[8], (r, 2 * g + core))
    local(outgoing.at[mine], tiles.at[mine], back_sem.at[8])
    drain(outgoing.at[pl.ds(0, 7)], back_sem.at[7])
    drain(tiles, back_sem.at[8])
    tri_ln = standardize(tiles[...].reshape(Z, B * B), 0).astype(BF)
    update = lax.dot_general(
        tri_ln, w_last[...], (((0,), (0,)), ((), ())), preferred_element_type=F32
    )
    pair_new[...] = (mid[...].astype(F32) + (gate[...] * update).reshape(B, B, Z)).astype(BF)
    done = pltpu.make_async_copy(pair_new, pair_out, back_sem.at[9])
    done.start()
    done.wait()
    x_done.wait()


def spread(block, out, B):
    blocks = [block(k) for k in range(N)]
    for i in range(B):
        out[:, i, :] = jnp.concatenate([b[:, i * B : (i + 1) * B] for b in blocks], 1)


def like(shape, dtype=BF):
    return jax.ShapeDtypeStruct(shape, dtype)


def shards(x, pair, w_in, w_out, w_bias, w_sides, w_outer, w_tri, w_tri_out):
    core = lax.rem(lax.axis_index("col"), 2)
    S, B, C = x.shape
    Z = pair.shape[2]
    H = w_bias.shape[1]
    O = w_sides.shape[1] // 2
    G = B // 4
    SP = S * N
    R = B * N
    P = -(-B * B // 128)

    VM = pltpu.VMEM
    args = [x, pair, w_in, w_out, w_bias.T, w_sides.T, w_outer, w_tri, w_tri_out]
    return comm_call(
        block_body, "block", 1, [like((S, B, C)), like((B, B, Z))], args, 16,
        [*(VM(v.shape, BF) for v in args),
         VM((S, B, C), BF), VM((N, N, B * B), BF), VM((B, B, Z), BF), VM((B * B, Z), F32), VM((B, B, Z), BF),
         VM((S, 2, 8, B, C), BF), VM((P, H, 128), BF), VM((N, H, 128), BF), VM((P, N, H, 128), BF), VM((H, B, R), F32),
         VM((S, B, C), F32), VM((S * B, C), F32), VM((S, R, C), BF), VM((S, H * B, R), F32),
         VM((S * B, C), F32),
         VM((S * B, 128), F32), VM((S, G, 4 * O), BF), VM((S, G, 4 * O), BF), VM((8, G, 4 * O), BF),
         VM((2, S, 8, G, 4 * O), BF), VM((2, S, 8, G, 4 * O), BF), VM((SP, G, 4 * O), F32),
         VM((SP, G, 4 * O), F32), VM((B * O, SP), F32), VM((10 * B, 4 * O * O), BF),
         VM((4 * O * O, 4 * Z), BF), VM((B * B, Z), F32), VM((8, N, B * B), BF), VM((8, N, B * B), BF),
         VM((8, B, R), F32), VM((N, B, R), BF), VM((2, 8, B, R), BF), VM((8, B, R), BF),
         VM((N, B, 8 * B), BF), VM((N, B, 8 * B), BF), VM((N, B, 8 * B), F32), VM((8, N, B * B), BF),
         VM((8, N, B * B), BF),
         pltpu.SemaphoreType.DMA((S,)), pltpu.SemaphoreType.DMA((S,)), pltpu.SemaphoreType.DMA((9,)),
         pltpu.SemaphoreType.DMA((10,))],
        pltpu.HBM,
    )


def solution(mesh):
    tile = PartitionSpec("row", "col", None)
    return jax.shard_map(
        shards,
        mesh=mesh,
        in_specs=(tile, tile) + (PartitionSpec(),) * 7,
        out_specs=(tile, tile),
        check_vma=False,
    )
```

time: 133 us -> 120 us (0.902)
  Pallas kernels: 126 us -> 116 us
  local copies, waits for them, and re-layouts: 5.98 us -> 3.38 us
    pallas_call x3 -> x1, Pallas kernels: 126 us -> 116 us  [comm_call(): pl.pallas_call(body, name=name, out_shape=outs, in_specs=[pl.BlockSpec(me...]
    unnamed x22 -> x2, local copies, waits for them, and re-layouts: 5.98 us -> 3.38 us
where the time goes in v4:
time: 120 us
  Pallas kernels  116 us (97%)
  local copies, waits for them, and re-layouts  3.38 us (3%)
    pallas_call x1, Pallas kernels, comm_call(): pl.pallas_call(body, name=name, out_shape=outs, in_specs=[pl.BlockSpec(me...  116 us
    unnamed x2, local copies, waits for them, and re-layouts  3.38 us

profile of v4, /device:TPU:8, one launch (start us, length us, event | category | flops | bytes accessed | tf_op | source)
XLA Modules:
  0.0 120.2 jit_solution(4662354016751676166)
XLA Ops:
  0.6 116.2 %block.1 = (bf16[8,40,256]{2,1,0:T(8,128)(2,1)}, bf16[40,40,128]{2,1,0:T(8,128)(2,1)}) custom-call(bf16[8,40,256]{2,1,0:T(8,128)(2,1)} %x_in.1, bf16[40,40,128]{2,1,0:T(8,128)(2,1)} %pair_in.1, bf16[256,1024]{1,0:T(8,128)(2,1)} %w_in_in.1, bf16[256,256]{1,0:T(8,128)(2,1)} %w_out_in.1, bf16[8,128]{1,0:T(8,128)(2,1)} %bitcast.3, bf16[64,256]{1,0:T(8,128)(2,1)} %bitcast.2, ...), custom_call_target="tpu_custom_call" | custom-call | tf_op jit(solution)/shard_map/block/pallas_call | solution.py:49
  116.8 1.6 %copy.13 = bf16[8,40,256]{2,1,0:T(8,128)(2,1)} copy(bf16[8,40,256]{2,1,0:T(8,128)(2,1)} %get-tuple-element.4) | data formatting | bytes 327680
  118.4 1.8 %copy.14 = bf16[40,40,128]{2,1,0:T(8,128)(2,1)} copy(bf16[40,40,128]{2,1,0:T(8,128)(2,1)} %get-tuple-element.5) | data formatting | bytes 819200

commit v5 on v4

--- a/solution.py
+++ b/solution.py
@@ -10,6 +10,8 @@
 MESH = pl.DeviceIdType.MESH
 EPS = 1e-05
 N = 16
+AROUND = (1, 7, 2, 6, 3, 5, 4, 0)
+AROUND_16 = (1, 15, 2, 14, 3, 13, 4, 12, 5, 11, 6, 10, 7, 9, 8)
 BF = jnp.bfloat16
 F32 = jnp.float32
 
@@ -65,9 +67,12 @@
     x, pair, w_in, w_out, w_bias, w_sides, w_outer, w_tri, w_last,
     x_new, got, mid, gate, pair_new, xs, bias_out, bias_in, biases, bias, q_all, gates, v_all, scores_all, gated,
     flat, left, right, chunk, lefts, rights, left_s, right_s, tall, stacked, w_wide, normed,
-    left_edge, right_edge, spreads, parts, held, mates, sums, channel, back, outgoing, tiles,
+    left_edge, right_edge, spreads, parts, held, mates, sums_0, sums_1, channel_0, channel_1, back_0, back_1,
+    outgoing_0, outgoing_1, tiles_0, tiles_1,
     near, far, load, back_sem, sem,
 ):
+    sums, channel, back = (sums_0, sums_1), (channel_0, channel_1), (back_0, back_1)
+    outgoing, tiles = (outgoing_0, outgoing_1), (tiles_0, tiles_1)
     r, c = here()
     core = lax.rem(c, 2)
     mate = c + 1 - 2 * core
@@ -138,14 +143,14 @@
 
     @pl.loop(0, S)
     def _(s):
-        for g in range(1, 8):
+        for g in AROUND[:-1]:
             push(x_in.at[s], xs.at[s, core, mine], sem.at[12], near.at[s], (r, lax.rem(c + 2 * g, N)))
         local(x_in.at[s], xs.at[s, core, mine], near.at[s])
 
     @pl.when(r < P)
     def _():
         drain(bias_in, sem.at[11])
-        for s in range(1, N):
+        for s in AROUND_16:
             push(bias_in, biases.at[r], sem.at[4], sem.at[5], (lax.rem(r + s, N), c))
         local(bias_in, biases.at[r], sem.at[5])
 
@@ -248,13 +253,13 @@
 
         part = right.at[pl.ds(first, count)]
         there = rights.at[parity, pl.ds(first, count), r // 2]
-        for s in range(1, N):
+        for s in AROUND_16:
             push(part, there, sem.at[2], sem.at[3], (lax.rem(r + s, N), c))
         local(part, there, sem.at[3])
     x_done = pltpu.make_async_copy(x_new, x_out, load.at[0])
     x_done.start()
     drain(chunk, sem.at[1])
-    for s in range(1, 8):
+    for s in AROUND[:-1]:
         push(chunk, lefts.at[core, mine], sem.at[6], sem.at[7], (r, lax.rem(c + 2 * s, N)))
     local(chunk, lefts.at[core, mine], sem.at[7])
     for g in range(7):
@@ -300,34 +305,41 @@
     def edge(k):
         w = w_tri[:, 2 * k * Z : 2 * (k + 1) * Z]
         both = lax.dot_general(w, tri_n, (((0,), (1,)), ((), ())), preferred_element_type=F32)
-        return (jax.nn.sigmoid(both[Z:]) * both[:Z]).astype(BF).reshape(8, N, B * B)
-
-    for k, ref in ((0, left_edge), (1, right_edge)):
-        ref[...] = edge(k)
-        for s in range(8):
-            g = lax.rem(c // 2 + s, 8)
+        return (jax.nn.sigmoid(both[Z:]) * both[:Z]).reshape(8, 2, 8, B * B)
+
+    def over_col(k, h):
+        ref = (left_edge, right_edge)[k]
+        for s in AROUND:
+            g = lax.rem(mine + s, 8)
             to = 2 * g + lax.rem(parity + 1 + k, 2)
             if s == 0:
 
                 @pl.when(to != c)
                 def _():
-                    push(ref.at[g], got.at[c], sem.at[14], sem.at[15], (r, to))
+                    push(ref.at[h, g], got.at[h, c], back_sem.at[14], back_sem.at[15 + h], (r, to))
 
                 @pl.when(to == c)
                 def _():
-                    local(ref.at[g], got.at[c], sem.at[15])
+                    local(ref.at[h, g], got.at[h, c], back_sem.at[15 + h])
             else:
-                push(ref.at[g], got.at[c], sem.at[14], sem.at[15], (r, to))
+                push(ref.at[h, g], got.at[h, c], back_sem.at[14], back_sem.at[15 + h], (r, to))
+
+    for k, ref in ((0, left_edge), (1, right_edge)):
+        values = edge(k)
+        for h in range(2):
+            ref[h] = values[:, h].astype(BF)
+        over_col(k, 0)
+    over_col(0, 1)
+    over_col(1, 1)
     gate[...] = jax.nn.sigmoid(jnp.dot(tri_n, w_tri[:, 4 * Z :], preferred_element_type=F32))
-    drain(got.at[pl.ds(0, N - 1)], sem.at[14])
-    drain(got, sem.at[15])
     kind = lax.rem(r + core, 2)
     R = N * B
+    arrived = back_sem.at[1 + 2 * parity + r // 8]
     for h in range(2):
-        spread(lambda k: got[k].astype(F32)[8 * h : 8 * h + 8], spreads, B)
+        drain(got.at[h], back_sem.at[15 + h])
+        spread(lambda k: got[h, k].astype(F32), spreads, B)
         parts[pl.ds(8 * h, 8)] = spreads[...].astype(BF)
-        arrived = back_sem.at[1 + lax.rem(r, 2)]
-        for s in range(8):
+        for s in AROUND:
             q = 8 * h + lax.rem(r + s, 8)
             if s == 0:
 
@@ -340,47 +352,74 @@
                     local(parts.at[q], held.at[kind, r // 2], arrived)
             else:
                 push(parts.at[q], held.at[kind, r // 2], back_sem.at[0], arrived, (q, c))
-    drain(held.at[1], back_sem.at[2 - core])
-    push(held.at[1], mates, back_sem.at[3], back_sem.at[4], (r, mate))
-    drain(held.at[0], back_sem.at[1 + core])
+    for h in range(2):
+        some = held.at[1, pl.ds(4 * h, 4)]
+        drain(some, back_sem.at[3 - 2 * core + h])
+        push(some, mates.at[pl.ds(4 * h, 4)], back_sem.at[5], back_sem.at[6], (r, mate))
+    for h in range(2):
+        drain(held.at[0, pl.ds(4 * h, 4)], back_sem.at[1 + 2 * core + h])
     columns = held[0].reshape(8 * B, R)
-    for rows, parity in ((held.at[1], 1 - core), (mates, core)):
-        if rows is mates:
-            drain(mates, back_sem.at[4])
-        total = lax.dot_general(
-            rows[...].reshape(8 * B, R), columns, (((1,), (1,)), ((), ())), preferred_element_type=F32
-        )
-        for s in range(8):
-            q = 2 * s + parity
-            sums[q] = total[s * B : (s + 1) * B].astype(BF)
+    rows = ((0, B * 3 // 5), (B * 3 // 5, B))
+
+    def products(ref):
+        return lax.dot_general(
+            ref.reshape(8 * B, R), columns, (((1,), (1,)), ((), ())), preferred_element_type=F32
+        )
+
+    def over_row(piece, odd):
+        for s in AROUND:
+            q = 2 * lax.rem(r // 2 + s, 8) + odd
 
             @pl.when(q != r)
             def _():
-                push(sums.at[q], channel.at[r], back_sem.at[5], back_sem.at[6], (q, c))
+                push(sums[piece].at[q], channel[piece].at[r], back_sem.at[7], back_sem.at[8 + piece], (q, c))
 
             @pl.when(q == r)
             def _():
-                local(sums.at[q], channel.at[r], back_sem.at[6])
+                local(sums[piece].at[q], channel[piece].at[r], back_sem.at[8 + piece])
+
+    for ref, odd in ((held.at[1], 1 - core), (mates, core)):
+        if ref is mates:
+            drain(mates, back_sem.at[6])
+        total = products(ref[...])
+        for piece, (low, high) in enumerate(rows):
+            for s in range(8):
+                sums[piece][2 * s + odd] = total[s * B + low : s * B + high].astype(BF)
+            if piece == 0:
+                over_row(0, odd)
+    over_row(1, 1 - core)
+    over_row(1, core)
     drain(parts.at[pl.ds(0, N - 1)], back_sem.at[0])
-    drain(mates, back_sem.at[3])
-    drain(sums.at[pl.ds(0, N - 1)], back_sem.at[5])
-    drain(channel, back_sem.at[6])
-    back[...] = channel[...].astype(F32)
-    rows = [back[:, i, :] for i in range(B)]
-    for g in range(8):
-        outgoing[g] = jnp.concatenate([v[:, g * B : (g + 1) * B] for v in rows], 1).astype(BF)
-    for s in range(1, 8):
-        g = lax.rem(mine + s, 8)
-        push(outgoing.at[g], tiles.at[mine], back_sem.at[7], back_sem.at[8], (r, 2 * g + core))
-    local(outgoing.at[mine], tiles.at[mine], back_sem.at[8])
-    drain(outgoing.at[pl.ds(0, 7)], back_sem.at[7])
-    drain(tiles, back_sem.at[8])
-    tri_ln = standardize(tiles[...].reshape(Z, B * B), 0).astype(BF)
-    update = lax.dot_general(
-        tri_ln, w_last[...], (((0,), (0,)), ((), ())), preferred_element_type=F32
-    )
-    pair_new[...] = (mid[...].astype(F32) + (gate[...] * update).reshape(B, B, Z)).astype(BF)
-    done = pltpu.make_async_copy(pair_new, pair_out, back_sem.at[9])
+    drain(mates, back_sem.at[5])
+    for piece in range(2):
+        drain(channel[piece], back_sem.at[8 + piece])
+        back[piece][...] = channel[piece][...].astype(F32)
+        lines = [back[piece][:, i, :] for i in range(back[piece].shape[1])]
+        for g in range(8):
+            outgoing[piece][g] = jnp.concatenate([v[:, g * B : (g + 1) * B] for v in lines], 1).astype(BF)
+        for s in AROUND[:-1]:
+            g = lax.rem(mine + s, 8)
+            push(
+                outgoing[piece].at[g], tiles[piece].at[mine], back_sem.at[10], back_sem.at[11 + piece],
+                (r, 2 * g + core),
+            )
+        local(outgoing[piece].at[mine], tiles[piece].at[mine], back_sem.at[11 + piece])
+    for piece, (low, high) in enumerate(rows):
+        drain(tiles[piece], back_sem.at[11 + piece])
+        tri_ln = standardize(tiles[piece][...].reshape(Z, (high - low) * B), 0).astype(BF)
+        update = lax.dot_general(
+            tri_ln, w_last[...], (((0,), (0,)), ((), ())), preferred_element_type=F32
+        )
+        pair_new[low:high] = (
+            mid[low:high].astype(F32)
+            + (gate[low * B : high * B, :] * update).reshape(high - low, B, Z)
+        ).astype(BF)
+    for piece in range(2):
+        drain(sums[piece].at[pl.ds(0, N - 1)], back_sem.at[7])
+        drain(outgoing[piece].at[pl.ds(0, 7)], back_sem.at[10])
+    for h in range(2):
+        drain(got.at[h, pl.ds(0, N - 1)], back_sem.at[14])
+    done = pltpu.make_async_copy(pair_new, pair_out, back_sem.at[13])
     done.start()
     done.wait()
     x_done.wait()
@@ -406,25 +445,26 @@
     SP = S * N
     R = B * N
     P = -(-B * B // 128)
+    pieces = (B * 3 // 5, B - B * 3 // 5)
 
     VM = pltpu.VMEM
     args = [x, pair, w_in, w_out, w_bias.T, w_sides.T, w_outer, w_tri, w_tri_out]
     return comm_call(
         block_body, "block", 1, [like((S, B, C)), like((B, B, Z))], args, 16,
         [*(VM(v.shape, BF) for v in args),
-         VM((S, B, C), BF), VM((N, N, B * B), BF), VM((B, B, Z), BF), VM((B * B, Z), F32), VM((B, B, Z), BF),
+         VM((S, B, C), BF), VM((2, N, 8, B * B), BF), VM((B, B, Z), BF), VM((B * B, Z), F32), VM((B, B, Z), BF),
          VM((S, 2, 8, B, C), BF), VM((P, H, 128), BF), VM((N, H, 128), BF), VM((P, N, H, 128), BF), VM((H, B, R), F32),
          VM((S, B, C), F32), VM((S * B, C), F32), VM((S, R, C), BF), VM((S, H * B, R), F32),
          VM((S * B, C), F32),
          VM((S * B, 128), F32), VM((S, G, 4 * O), BF), VM((S, G, 4 * O), BF), VM((8, G, 4 * O), BF),
          VM((2, S, 8, G, 4 * O), BF), VM((2, S, 8, G, 4 * O), BF), VM((SP, G, 4 * O), F32),
          VM((SP, G, 4 * O), F32), VM((B * O, SP), F32), VM((10 * B, 4 * O * O), BF),
-         VM((4 * O * O, 4 * Z), BF), VM((B * B, Z), F32), VM((8, N, B * B), BF), VM((8, N, B * B), BF),
+         VM((4 * O * O, 4 * Z), BF), VM((B * B, Z), F32), VM((2, 8, 8, B * B), BF), VM((2, 8, 8, B * B), BF),
          VM((8, B, R), F32), VM((N, B, R), BF), VM((2, 8, B, R), BF), VM((8, B, R), BF),
-         VM((N, B, 8 * B), BF), VM((N, B, 8 * B), BF), VM((N, B, 8 * B), F32), VM((8, N, B * B), BF),
-         VM((8, N, B * B), BF),
+         *(VM((N, n, 8 * B), t) for t in (BF, BF, F32) for n in pieces),
+         *(VM((8, N, n * B), BF) for _ in range(2) for n in pieces),
          pltpu.SemaphoreType.DMA((S,)), pltpu.SemaphoreType.DMA((S,)), pltpu.SemaphoreType.DMA((9,)),
-         pltpu.SemaphoreType.DMA((10,))],
+         pltpu.SemaphoreType.DMA((17,))],
         pltpu.HBM,
     )
 

time: 120 us -> 118 us (0.983)
  Pallas kernels: 116 us -> 114 us
    pallas_call x1, Pallas kernels: 116 us -> 114 us  [comm_call(): pl.pallas_call(body, name=name, out_shape=outs, in_specs=[pl.BlockSpec(me...]
where the time goes in v5:
time: 118 us
  Pallas kernels  114 us (97%)
  local copies, waits for them, and re-layouts  3.38 us (3%)
    pallas_call x1, Pallas kernels, comm_call(): pl.pallas_call(body, name=name, out_shape=outs, in_specs=[pl.BlockSpec(me...  114 us
    unnamed x2, local copies, waits for them, and re-layouts  3.38 us

profile of v5, /device:TPU:8, one launch (start us, length us, event | category | flops | bytes accessed | tf_op | source)
XLA Modules:
  0.0 117.9 jit_solution(5996071057633417308)
XLA Ops:
  0.6 113.9 %block.1 = (bf16[8,40,256]{2,1,0:T(8,128)(2,1)}, bf16[40,40,128]{2,1,0:T(8,128)(2,1)}) custom-call(bf16[8,40,256]{2,1,0:T(8,128)(2,1)} %x_in.1, bf16[40,40,128]{2,1,0:T(8,128)(2,1)} %pair_in.1, bf16[256,1024]{1,0:T(8,128)(2,1)} %w_in_in.1, bf16[256,256]{1,0:T(8,128)(2,1)} %w_out_in.1, bf16[8,128]{1,0:T(8,128)(2,1)} %bitcast.3, bf16[64,256]{1,0:T(8,128)(2,1)} %bitcast.2, ...), custom_call_target="tpu_custom_call" | custom-call | tf_op jit(solution)/shard_map/block/pallas_call | solution.py:51
  114.5 1.6 %copy.13 = bf16[8,40,256]{2,1,0:T(8,128)(2,1)} copy(bf16[8,40,256]{2,1,0:T(8,128)(2,1)} %get-tuple-element.4) | data formatting | bytes 327680
  116.1 1.8 %copy.14 = bf16[40,40,128]{2,1,0:T(8,128)(2,1)} copy(bf16[40,40,128]{2,1,0:T(8,128)(2,1)} %get-tuple-element.5) | data formatting | bytes 819200

commit v6 on v5

--- a/solution.py
+++ b/solution.py
@@ -69,7 +69,7 @@
     flat, left, right, chunk, lefts, rights, left_s, right_s, tall, stacked, w_wide, normed,
     left_edge, right_edge, spreads, parts, held, mates, sums_0, sums_1, channel_0, channel_1, back_0, back_1,
     outgoing_0, outgoing_1, tiles_0, tiles_1,
-    near, far, load, back_sem, sem,
+    near, far, aside, across, load, back_sem, sem,
 ):
     sums, channel, back = (sums_0, sums_1), (channel_0, channel_1), (back_0, back_1)
     outgoing, tiles = (outgoing_0, outgoing_1), (tiles_0, tiles_1)
@@ -77,6 +77,9 @@
     core = lax.rem(c, 2)
     mate = c + 1 - 2 * core
     mine = c // 2
+    beside = mine + 1 - 2 * lax.rem(mine, 2)
+    opposite = lax.rem(mine + 4, 8)
+    ahead, behind = lax.rem(c + 4, N), lax.rem(c + 12, N)
     parity = lax.rem(r, 2)
     S, B, C = x.shape
     H = w_bias.shape[0]
@@ -143,8 +146,11 @@
 
     @pl.loop(0, S)
     def _(s):
-        for g in AROUND[:-1]:
-            push(x_in.at[s], xs.at[s, core, mine], sem.at[12], near.at[s], (r, lax.rem(c + 2 * g, N)))
+        block = xs.at[s, core, mine]
+        push(x_in.at[s], block, sem.at[12], aside.at[s], (r, 2 * beside + core))
+        push(x_in.at[s], block, sem.at[12], across.at[s], (r, 2 * opposite + core))
+        for to in (ahead, behind):
+            push(x_in.at[s], block, sem.at[12], near.at[s], (r, to))
         local(x_in.at[s], xs.at[s, core, mine], near.at[s])
 
     @pl.when(r < P)
@@ -154,8 +160,17 @@
             push(bias_in, biases.at[r], sem.at[4], sem.at[5], (lax.rem(r + s, N), c))
         local(bias_in, biases.at[r], sem.at[5])
 
+    def relay(s):
+        block = xs.at[s, core, beside]
+        drain(block, aside.at[s])
+        for to in (ahead, behind):
+            push(block, block, sem.at[12], near.at[s], (r, to))
+        block = xs.at[s, core, opposite]
+        drain(block, across.at[s])
+        push(block, block, sem.at[12], near.at[s], (r, 2 * beside + core))
+
     def forward(s):
-        drain(xs.at[s, core], near.at[s])
+        drain(xs.at[s, core, pl.ds(0, 6)], near.at[s])
         push(xs.at[s, core], xs.at[s, core], sem.at[13], far.at[s], (r, mate))
 
     for cp in loads[2:]:
@@ -171,10 +186,16 @@
         for i in range(4):
             w_wide[pl.ds(d * 4 * O + i * O, O), i * Z : (i + 1) * Z] = part
     head = lax.broadcasted_iota(jnp.int32, (B, C), 1) // D
+    relay(0)
+    relay(1)
     forward(0)
 
     @pl.loop(0, S)
     def _(s):
+        @pl.when(s < S - 2)
+        def _():
+            relay(s + 2)
+
         @pl.when(s < S - 1)
         def _():
             forward(s + 1)
@@ -463,7 +484,7 @@
          VM((8, B, R), F32), VM((N, B, R), BF), VM((2, 8, B, R), BF), VM((8, B, R), BF),
          *(VM((N, n, 8 * B), t) for t in (BF, BF, F32) for n in pieces),
          *(VM((8, N, n * B), BF) for _ in range(2) for n in pieces),
-         pltpu.SemaphoreType.DMA((S,)), pltpu.SemaphoreType.DMA((S,)), pltpu.SemaphoreType.DMA((9,)),
+         *(pltpu.SemaphoreType.DMA((S,)) for _ in range(4)), pltpu.SemaphoreType.DMA((9,)),
          pltpu.SemaphoreType.DMA((17,))],
         pltpu.HBM,
     )

time: 118 us -> 119 us (level)
  no operation moved by 1% of the time
where the time goes in v6:
time: 119 us; the launch traced here: 118 us
  Pallas kernels  114 us (96%)
  local copies, waits for them, and re-layouts  3.38 us (3%)
    pallas_call x1, Pallas kernels, comm_call(): pl.pallas_call(body, name=name, out_shape=outs, in_specs=[pl.BlockSpec(me...  114 us
    unnamed x2, local copies, waits for them, and re-layouts  3.38 us

profile of v6, /device:TPU:8, one launch (start us, length us, event | category | flops | bytes accessed | tf_op | source)
XLA Modules:
  0.0 118.3 jit_solution(13748927480217421989)
XLA Ops:
  0.6 114.2 %block.1 = (bf16[8,40,256]{2,1,0:T(8,128)(2,1)}, bf16[40,40,128]{2,1,0:T(8,128)(2,1)}) custom-call(bf16[8,40,256]{2,1,0:T(8,128)(2,1)} %x_in.1, bf16[40,40,128]{2,1,0:T(8,128)(2,1)} %pair_in.1, bf16[256,1024]{1,0:T(8,128)(2,1)} %w_in_in.1, bf16[256,256]{1,0:T(8,128)(2,1)} %w_out_in.1, bf16[8,128]{1,0:T(8,128)(2,1)} %bitcast.3, bf16[64,256]{1,0:T(8,128)(2,1)} %bitcast.2, ...), custom_call_target="tpu_custom_call" | custom-call | tf_op jit(solution)/shard_map/block/pallas_call | solution.py:51
  114.9 1.6 %copy.13 = bf16[8,40,256]{2,1,0:T(8,128)(2,1)} copy(bf16[8,40,256]{2,1,0:T(8,128)(2,1)} %get-tuple-element.4) | data formatting | bytes 327680
  116.5 1.8 %copy.14 = bf16[40,40,128]{2,1,0:T(8,128)(2,1)} copy(bf16[40,40,128]{2,1,0:T(8,128)(2,1)} %get-tuple-element.5) | data formatting | bytes 819200

commit v7 on v5

--- a/solution.py
+++ b/solution.py
@@ -210,7 +210,7 @@
     for half in range(2):
         first, count = half * S // 2, S // 2
 
-        @pl.loop(first, first + count)
+        @pl.loop(first, first + count, unroll=2)
         def _(s):
             scores = scores_all[s] + bias[...].reshape(H * B, N * B)
             e = jnp.exp(scores - jnp.max(scores, -1, keepdims=True))

time: 118 us -> 118 us (level)
  no operation moved by 1% of the time
where the time goes in v7:
time: 118 us
  Pallas kernels  114 us (97%)
  local copies, waits for them, and re-layouts  3.38 us (3%)
    pallas_call x1, Pallas kernels, comm_call(): pl.pallas_call(body, name=name, out_shape=outs, in_specs=[pl.BlockSpec(me...  114 us
    unnamed x2, local copies, waits for them, and re-layouts  3.38 us

profile of v7, /device:TPU:8, one launch (start us, length us, event | category | flops | bytes accessed | tf_op | source)
XLA Modules:
  0.0 117.9 jit_solution(4408162221823085275)
XLA Ops:
  0.6 113.8 %block.1 = (bf16[8,40,256]{2,1,0:T(8,128)(2,1)}, bf16[40,40,128]{2,1,0:T(8,128)(2,1)}) custom-call(bf16[8,40,256]{2,1,0:T(8,128)(2,1)} %x_in.1, bf16[40,40,128]{2,1,0:T(8,128)(2,1)} %pair_in.1, bf16[256,1024]{1,0:T(8,128)(2,1)} %w_in_in.1, bf16[256,256]{1,0:T(8,128)(2,1)} %w_out_in.1, bf16[8,128]{1,0:T(8,128)(2,1)} %bitcast.3, bf16[64,256]{1,0:T(8,128)(2,1)} %bitcast.2, ...), custom_call_target="tpu_custom_call" | custom-call | tf_op jit(solution)/shard_map/block/pallas_call | solution.py:51
  114.5 1.6 %copy.13 = bf16[8,40,256]{2,1,0:T(8,128)(2,1)} copy(bf16[8,40,256]{2,1,0:T(8,128)(2,1)} %get-tuple-element.4) | data formatting | bytes 327680
  116.1 1.8 %copy.14 = bf16[40,40,128]{2,1,0:T(8,128)(2,1)} copy(bf16[40,40,128]{2,1,0:T(8,128)(2,1)} %get-tuple-element.5) | data formatting | bytes 819200

commit v8 on v5

--- a/solution.py
+++ b/solution.py
@@ -207,8 +207,7 @@
         return jnp.concatenate([biases[p, block].astype(F32) for p in range(P)], 1)
 
     spread(bias_of, bias, B)
-    for half in range(2):
-        first, count = half * S // 2, S // 2
+    for first, count in ((0, 3 * S // 4), (3 * S // 4, S // 4)):
 
         @pl.loop(first, first + count)
         def _(s):

time: 118 us -> 123 us (1.042)
  Pallas kernels: 114 us -> 118 us
    pallas_call x1, Pallas kernels: 114 us -> 118 us  [comm_call(): pl.pallas_call(body, name=name, out_shape=outs, in_specs=[pl.BlockSpec(me...]
where the time goes in v8:
time: 123 us; the launch traced here: 122 us
  Pallas kernels  118 us (96%)
  local copies, waits for them, and re-layouts  3.38 us (3%)
    pallas_call x1, Pallas kernels, comm_call(): pl.pallas_call(body, name=name, out_shape=outs, in_specs=[pl.BlockSpec(me...  118 us
    unnamed x2, local copies, waits for them, and re-layouts  3.38 us

profile of v8, /device:TPU:8, one launch (start us, length us, event | category | flops | bytes accessed | tf_op | source)
XLA Modules:
  0.0 122.1 jit_solution(3750940437160126913)
XLA Ops:
  0.6 118.1 %block.1 = (bf16[8,40,256]{2,1,0:T(8,128)(2,1)}, bf16[40,40,128]{2,1,0:T(8,128)(2,1)}) custom-call(bf16[8,40,256]{2,1,0:T(8,128)(2,1)} %x_in.1, bf16[40,40,128]{2,1,0:T(8,128)(2,1)} %pair_in.1, bf16[256,1024]{1,0:T(8,128)(2,1)} %w_in_in.1, bf16[256,256]{1,0:T(8,128)(2,1)} %w_out_in.1, bf16[8,128]{1,0:T(8,128)(2,1)} %bitcast.3, bf16[64,256]{1,0:T(8,128)(2,1)} %bitcast.2, ...), custom_call_target="tpu_custom_call" | custom-call | tf_op jit(solution)/shard_map/block/pallas_call | solution.py:51
  118.8 1.6 %copy.13 = bf16[8,40,256]{2,1,0:T(8,128)(2,1)} copy(bf16[8,40,256]{2,1,0:T(8,128)(2,1)} %get-tuple-element.4) | data formatting | bytes 327680
  120.3 1.8 %copy.14 = bf16[40,40,128]{2,1,0:T(8,128)(2,1)} copy(bf16[40,40,128]{2,1,0:T(8,128)(2,1)} %get-tuple-element.5) | data formatting | bytes 819200
